TPU v7x, 32 devices: a whole 2x2x4 slice. The times are simulated.
32 devices in a mesh: section: 4 (over y, x), dp: 8 (over z, core).
Axes of the slice: x: 2, y: 2, z: 4, core: 2. Of those that a mesh axis runs over, the one named last changes fastest.
Arguments:
- patches: bfloat16 [32, 256, 768], P(('section', 'dp')), may hold values from -6 to 6
- cotangent: bfloat16 [32, 256, 768], P(('section', 'dp')), may hold values from -6 to 6
- positions: int32 [32, 2, 256], P(('section', 'dp')), may hold values from 0 to 15, as said below
- kept_counts: int32 [32], P(('section', 'dp')), may hold values from 32 to 256, as said below
- norm_gain: float32 [4, 768], P('section'), may hold values from 0.5 to 1.5
- norm_bias: float32 [4, 768], P('section'), may hold values from -4 to 4
- w_main: bfloat16 [4, 768, 3072], P('section')
- b_main: float32 [4, 3072], P('section'), may hold values from -4 to 4
- section_vector: float32 [4, 768], P('section')
- w_down: bfloat16 [4, 1536, 768], P('section'), may hold values from -0.109375 to 0.109375
Outputs:
- outputs: bfloat16 [32, 256, 768], P(('section', 'dp'))
- input_grad: bfloat16 [32, 256, 768], P(('section', 'dp'))
- grad_norm_gain: float32 [4, 768], P('section')
- grad_norm_bias: float32 [4, 768], P('section')
- grad_w_main: float32 [4, 768, 3072], P('section')
- grad_b_main: float32 [4, 3072], P('section')
- grad_section_vector: float32 [4, 768], P('section')
- grad_w_down: float32 [4, 1536, 768], P('section')
Inputs may be any that keep to these rules, and one draw needn't show every extreme that they name: `positions`: an image's first kept_counts slots hold its kept patches in raster order, the other slots its dropped patches in raster order; no patch appears twice in an image. `kept_counts`: some image keeps all 256 slots.
All inputs are finite; a program needn't handle non-finite values.
Results may differ from a plain program's by a relative error of at most 0.02.
Values may be sent and summed in bfloat16 or wider, within the bound.
A program may use at most 448 MiB of HBM per device.

v0:
```python
import jax
import jax.numpy as jnp
from jax import lax
from jax.sharding import PartitionSpec as P

HEADS = 12
HEAD_DIM = 64


def shifted(x, axis, by):
    length = lax.axis_size(axis)
    pairs = [(i, i + by) for i in range(length) if 0 <= i + by < length]
    return lax.ppermute(x, axis, pairs)


def layer_norm(values, norm_scale, norm_offset):
    average = jnp.mean(values, axis=-1, keepdims=True)
    centered = values - average
    spread = jnp.mean(centered * centered, axis=-1, keepdims=True)
    return centered * lax.rsqrt(spread + 1e-06) * norm_scale + norm_offset


def exact_gelu(values):
    return jax.nn.gelu(values, approximate=False)


def rotate(tensor, cosine, sine_part):
    half_width = tensor.shape[-1] // 2
    first_half = tensor[..., :half_width]
    second_half = tensor[..., half_width:]
    return jnp.concatenate(
        [
            first_half * cosine - second_half * sine_part,
            first_half * sine_part + second_half * cosine,
        ],
        axis=-1,
    )


def mixer_core(hidden, token_table, params):
    valid_mask, grid_rows, grid_cols = token_table
    norm_scale, norm_offset, matrix, biases, section_extra, down_full = params
    images, length, model_width = hidden.shape
    rows_all = images * length
    half_width = HEAD_DIM // 2
    score_scale = HEAD_DIM ** (-0.5)
    normed, norm_pull = jax.vjp(layer_norm, hidden, norm_scale, norm_offset)
    normed_low = normed.astype(jnp.bfloat16).reshape(rows_all, model_width)
    project = (
        jnp.dot(normed_low, matrix[:, : 3 * model_width], preferred_element_type=jnp.float32)
        + biases[: 3 * model_width]
    )
    project = project.reshape(images, length, 3, HEADS, HEAD_DIM)

    def rotate_both(query_in, key_in, freq_in):
        freq_rows = freq_in[: model_width // 2].reshape(HEADS, half_width)
        freq_cols = freq_in[model_width // 2 :].reshape(HEADS, half_width)
        angles = grid_rows[:, :, None, None] * freq_rows + grid_cols[:, :, None, None] * freq_cols
        cosine = jnp.cos(angles)
        sine_part = jnp.sin(angles)
        return (rotate(query_in, cosine, sine_part), rotate(key_in, cosine, sine_part))

    rotated, rotate_pull = jax.vjp(rotate_both, project[:, :, 0], project[:, :, 1], section_extra)
    query_low = rotated[0].astype(jnp.bfloat16)
    key_low = rotated[1].astype(jnp.bfloat16)
    value_low = project[:, :, 2].astype(jnp.bfloat16)
    scores = (
        jnp.einsum("gqhe,gkhe->ghqk", query_low, key_low, preferred_element_type=jnp.float32)
        * score_scale
    )
    scores = jnp.where(valid_mask[:, None, None, :] > 0.5, scores, -1e30)
    attn_probs = jax.nn.softmax(scores, axis=-1)
    weights_low = attn_probs.astype(jnp.bfloat16)
    context = jnp.einsum(
        "ghqk,gkhe->gqhe", weights_low, value_low, preferred_element_type=jnp.float32
    )
    context_low = context.reshape(rows_all, model_width).astype(jnp.bfloat16)
    return (
        normed_low,
        norm_pull,
        query_low,
        key_low,
        value_low,
        rotate_pull,
        attn_probs,
        weights_low,
        context_low,
    )


def mixer_forward(hidden, token_table, params):
    matrix, biases = (params[2], params[3])
    images, length, model_width = hidden.shape
    context_low = mixer_core(hidden, token_table, params)[8]
    branch = (
        jnp.dot(context_low, matrix[:, 3 * model_width :], preferred_element_type=jnp.float32)
        + biases[3 * model_width :]
    )
    return hidden + token_table[0][..., None] * branch.reshape(images, length, model_width)


def mixer_backward(hidden, upstream, token_table, params):
    norm_scale, norm_offset, matrix, biases, section_extra, down_full = params
    images, length, model_width = hidden.shape
    rows_all = images * length
    score_scale = HEAD_DIM ** (-0.5)
    (
        normed_low,
        norm_pull,
        query_low,
        key_low,
        value_low,
        rotate_pull,
        attn_probs,
        weights_low,
        context_low,
    ) = mixer_core(hidden, token_table, params)
    branch_grad = (upstream * token_table[0][..., None]).reshape(rows_all, model_width)
    branch_low = branch_grad.astype(jnp.bfloat16)
    out_matrix = matrix[:, 3 * model_width :]
    grad_out_w = jnp.dot(context_low.T, branch_low, preferred_element_type=jnp.float32)
    grad_out_b = jnp.sum(branch_grad, axis=0)
    grad_context = jnp.dot(branch_low, out_matrix.T, preferred_element_type=jnp.float32).astype(
        jnp.bfloat16
    )
    grad_context = grad_context.reshape(images, length, HEADS, HEAD_DIM)
    grad_weights = jnp.einsum(
        "gqhe,gkhe->ghqk", grad_context, value_low, preferred_element_type=jnp.float32
    )
    grad_value = jnp.einsum(
        "ghqk,gqhe->gkhe", weights_low, grad_context, preferred_element_type=jnp.float32
    )
    grad_scores = attn_probs * (
        grad_weights - jnp.sum(attn_probs * grad_weights, axis=-1, keepdims=True)
    )
    grad_low = grad_scores.astype(jnp.bfloat16)
    grad_query = (
        jnp.einsum("ghqk,gkhe->gqhe", grad_low, key_low, preferred_element_type=jnp.float32)
        * score_scale
    )
    grad_key = (
        jnp.einsum("ghqk,gqhe->gkhe", grad_low, query_low, preferred_element_type=jnp.float32)
        * score_scale
    )
    grad_query_raw, grad_key_raw, grad_freq = rotate_pull((grad_query, grad_key))
    grad_project = (
        jnp.stack([grad_query_raw, grad_key_raw, grad_value], axis=2)
        .reshape(rows_all, 3 * model_width)
        .astype(jnp.bfloat16)
    )
    grad_in_w = jnp.dot(normed_low.T, grad_project, preferred_element_type=jnp.float32)
    grad_in_b = jnp.sum(grad_project.astype(jnp.float32), axis=0)
    grad_normed = jnp.dot(
        grad_project, matrix[:, : 3 * model_width].T, preferred_element_type=jnp.float32
    )
    grad_hidden, grad_gain, grad_offset = norm_pull(
        grad_normed.reshape(images, length, model_width)
    )
    gradients = (
        grad_gain,
        grad_offset,
        jnp.concatenate([grad_in_w, grad_out_w], axis=1),
        jnp.concatenate([grad_in_b, grad_out_b], axis=0),
        grad_freq,
        jnp.zeros(down_full.shape, jnp.float32),
    )
    return (upstream + grad_hidden, gradients)


def dense_core(hidden, params):
    norm_scale, norm_offset, matrix, biases, section_extra, down_full = params
    images, length, model_width = hidden.shape
    normed, norm_pull = jax.vjp(layer_norm, hidden, norm_scale, norm_offset)
    normed_low = normed.astype(jnp.bfloat16).reshape(images * length, model_width)
    pre_gelu = jnp.dot(normed_low, matrix, preferred_element_type=jnp.float32) + biases
    activated, gelu_pull = jax.vjp(exact_gelu, pre_gelu)
    return (normed_low, norm_pull, activated.astype(jnp.bfloat16), gelu_pull)


def dense_forward(hidden, token_table, params):
    images, length, model_width = hidden.shape
    hid_low = dense_core(hidden, params)[2]
    branch = jnp.dot(hid_low, params[5], preferred_element_type=jnp.float32) + params[4]
    return hidden + token_table[0][..., None] * branch.reshape(images, length, model_width)


def dense_backward(hidden, upstream, token_table, params):
    norm_scale, norm_offset, matrix, biases, section_extra, down_full = params
    images, length, model_width = hidden.shape
    rows_all = images * length
    normed_low, norm_pull, hid_low, gelu_pull = dense_core(hidden, params)
    branch_grad = (upstream * token_table[0][..., None]).reshape(rows_all, model_width)
    branch_low = branch_grad.astype(jnp.bfloat16)
    grad_down = jnp.dot(hid_low.T, branch_low, preferred_element_type=jnp.float32)
    grad_down_b = jnp.sum(branch_grad, axis=0)
    grad_hid = jnp.dot(branch_low, down_full.T, preferred_element_type=jnp.float32)
    grad_pre = gelu_pull(grad_hid)[0].astype(jnp.bfloat16)
    grad_in_w = jnp.dot(normed_low.T, grad_pre, preferred_element_type=jnp.float32)
    grad_in_b = jnp.sum(grad_pre.astype(jnp.float32), axis=0)
    grad_normed = jnp.dot(grad_pre, matrix.T, preferred_element_type=jnp.float32)
    grad_hidden, grad_gain, grad_offset = norm_pull(
        grad_normed.reshape(images, length, model_width)
    )
    return (
        upstream + grad_hidden,
        (grad_gain, grad_offset, grad_in_w, grad_in_b, grad_down_b, grad_down),
    )


def zero_gradients(params):
    return tuple((jnp.zeros(member.shape, jnp.float32) for member in params))


def spare_forward(hidden, token_table, params):
    return hidden


def spare_backward(hidden, upstream, token_table, params):
    return (upstream, zero_gradients(params))


def micro_table(fed_table, slot_index, images):
    part_rows = lax.dynamic_slice_in_dim(fed_table, slot_index * images, images, 0).astype(
        jnp.float32
    )
    return (part_rows[:, 0], part_rows[:, 1], part_rows[:, 2])


def on_device(
    patches,
    cotangent,
    positions,
    kept_counts,
    norm_gain,
    norm_bias,
    w_main,
    b_main,
    section_vector,
    w_down,
):
    sections = lax.axis_size("section")
    section_place = lax.axis_index("section")
    images, length, model_width = patches.shape
    slot_ids = jnp.arange(length, dtype=jnp.int32)
    valid_local = (slot_ids[None, :] < kept_counts[:, None]).astype(jnp.float32)
    table_local = jnp.stack(
        [
            valid_local,
            positions[:, 0, :].astype(jnp.float32),
            positions[:, 1, :].astype(jnp.float32),
        ],
        axis=1,
    ).astype(jnp.bfloat16)
    fed_patches, fed_cotangent, fed_table = (
        lax.all_gather(patches, "section", axis=0, tiled=True),
        lax.all_gather(cotangent, "section", axis=0, tiled=True),
        lax.all_gather(table_local, "section", axis=0, tiled=True),
    )
    fetched = shifted(w_down, "section", 1)[0]
    down_full = jnp.concatenate([fetched, w_down[0]], axis=0)
    params = (norm_gain[0], norm_bias[0], w_main[0], b_main[0], section_vector[0], down_full)
    is_mixer = section_place % 2 == 0
    section_kind = jnp.where(is_mixer, 1, 2).astype(jnp.int32)
    forward_fns = [spare_forward, mixer_forward, dense_forward]
    backward_fns = [spare_backward, mixer_backward, dense_backward]
    zero_act = jnp.zeros((images, length, model_width), jnp.bfloat16)
    incoming = zero_act
    saved = jnp.zeros((sections, images, length, model_width), jnp.bfloat16)
    produced = jnp.zeros((sections, images, length, model_width), jnp.bfloat16)
    for tick_index in range(2 * sections - 1):
        micro_index = tick_index - section_place
        is_live = (micro_index >= 0) & (micro_index < sections)
        slot_index = jnp.clip(micro_index, 0, sections - 1)
        if tick_index < sections:
            entering = fed_patches[tick_index * images : (tick_index + 1) * images]
        else:
            entering = zero_act
        section_in = jnp.where(section_place == 0, entering, incoming)
        previous = lax.dynamic_index_in_dim(saved, slot_index, 0, keepdims=False)
        saved = lax.dynamic_update_index_in_dim(
            saved, jnp.where(is_live, section_in, previous), slot_index, 0
        )
        token_table = micro_table(fed_table, slot_index, images)
        branch_index = jnp.where(is_live, section_kind, 0)
        section_out = lax.switch(
            branch_index, forward_fns, section_in.astype(jnp.float32), token_table, params
        ).astype(jnp.bfloat16)
        earlier = lax.dynamic_index_in_dim(produced, slot_index, 0, keepdims=False)
        produced = lax.dynamic_update_index_in_dim(
            produced, jnp.where(is_live, section_out, earlier), slot_index, 0
        )
        if tick_index < 2 * sections - 2:
            incoming = shifted(section_out, "section", 1)
    upstream_in = zero_act
    returned = jnp.zeros((sections, images, length, model_width), jnp.bfloat16)
    totals = zero_gradients(params)
    for tick_index in range(2 * sections - 1):
        micro_index = tick_index - (sections - 1 - section_place)
        is_live = (micro_index >= 0) & (micro_index < sections)
        slot_index = jnp.clip(micro_index, 0, sections - 1)
        if tick_index < sections:
            entering = fed_cotangent[tick_index * images : (tick_index + 1) * images]
        else:
            entering = zero_act
        grad_in = jnp.where(section_place == sections - 1, entering, upstream_in)
        section_saved = lax.dynamic_index_in_dim(saved, slot_index, 0, keepdims=False)
        token_table = micro_table(fed_table, slot_index, images)
        branch_index = jnp.where(is_live, section_kind, 0)
        grad_hidden, gradients = lax.switch(
            branch_index,
            backward_fns,
            section_saved.astype(jnp.float32),
            grad_in.astype(jnp.float32),
            token_table,
            params,
        )
        totals = tuple((running + addend for running, addend in zip(totals, gradients)))
        grad_low = grad_hidden.astype(jnp.bfloat16)
        earlier = lax.dynamic_index_in_dim(returned, slot_index, 0, keepdims=False)
        returned = lax.dynamic_update_index_in_dim(
            returned, jnp.where(is_live, grad_low, earlier), slot_index, 0
        )
        if tick_index < 2 * sections - 2:
            upstream_in = shifted(grad_low, "section", -1)
    results, input_grads = (
        lax.all_to_all(produced, "section", split_axis=0, concat_axis=0, tiled=True),
        lax.all_to_all(returned, "section", split_axis=0, concat_axis=0, tiled=True),
    )
    outputs = results[sections - 1]
    input_grad = input_grads[0]
    grad_gain, grad_offset, grad_matrix, grad_vector, grad_extra, grad_down = totals
    half_rows = grad_down.shape[0] // 2
    summed = (
        lax.psum(grad_gain.astype(jnp.bfloat16), "dp").astype(jnp.float32),
        lax.psum(grad_offset.astype(jnp.bfloat16), "dp").astype(jnp.float32),
        lax.psum(grad_matrix.astype(jnp.bfloat16), "dp").astype(jnp.float32),
        lax.psum(grad_vector.astype(jnp.bfloat16), "dp").astype(jnp.float32),
        lax.psum(grad_extra.astype(jnp.bfloat16), "dp").astype(jnp.float32),
        lax.psum(grad_down.astype(jnp.bfloat16), "dp").astype(jnp.float32),
    )
    lower_half = summed[5][:half_rows]
    upper_half = summed[5][half_rows:]
    returned_half = shifted(lower_half.astype(jnp.bfloat16), "section", -1).astype(lower_half.dtype)
    down_part = jnp.where(is_mixer, returned_half, upper_half)
    sum_gain, sum_offset, sum_matrix, sum_vector, sum_extra = (
        summed[0],
        summed[1],
        summed[2],
        summed[3],
        summed[4],
    )
    return (
        outputs,
        input_grad,
        sum_gain[None],
        sum_offset[None],
        sum_matrix[None],
        sum_vector[None],
        sum_extra[None],
        down_part[None],
    )


def solution(mesh):
    in_specs = (
        P(("section", "dp"), None, None),
        P(("section", "dp"), None, None),
        P(("section", "dp"), None, None),
        P(("section", "dp")),
        P("section", None),
        P("section", None),
        P("section", None, None),
        P("section", None),
        P("section", None),
        P("section", None, None),
    )
    out_specs = (
        P(("section", "dp"), None, None),
        P(("section", "dp"), None, None),
        P("section", None),
        P("section", None),
        P("section", None, None),
        P("section", None),
        P("section", None),
        P("section", None, None),
    )
    return jax.shard_map(
        on_device, mesh=mesh, in_specs=in_specs, out_specs=out_specs, check_vma=False
    )
```

profile of v0, /device:TPU:0, one launch (start us, length us, event | category | flops | bytes accessed | tf_op | source)
XLA Modules:
  0.0 1160.4 jit_solution(219394993217223267)
XLA Ops:
  7.9 5.0 collective-permute-start
  14.6 69.9 %all_gather.10 = bf16[4,3,256]{2,1,0:T(4,128)(2,1)S(1)} all-gather(bf16[1,3,256]{2,1,0:T(4,128)(2,1)S(1)} %pad_maximum_fusion.113), channel_id=1, replica_groups=mesh['section'=4,'dp'=8] {'section'}, dimensions={0}, use_global_device_ids=true | all-gather | bytes 7680 | tf_op jit(solution)/shard_map/all_gather | solution.py:257
  95.2 22.9 %conditional.14 = (f32[1,256,768]{2,1,0:T(8,128)S(1)}) conditional(s32[]{:T(128)} %clamp.42, f32[1,256,768]{2,1,0:T(8,128)S(1)} %fusion.1184, (f32[1,1,256]{2,1,0:T(1,128)S(1)}, f32[1,256,768]{2,1,0:T(8,128)S(1)}, f32[1,768]{1,0:T(1,128)S(1)}, f32[1,768]{1,0:T(1,128)S(1)}, bf16[768,3072]{1,0:T(8,128)(2,1)}, ...), branch_computations={%region_0.1_spmd, %region_1.6_spmd, %region_6.9_spmd} | conditional | flops 2470183168 | bytes 35926772 | solution.py:285
  99.4 4.6 convolution_add_fusion
  129.5 27.3 %conditional.15 = (f32[1,256,768]{2,1,0:T(8,128)S(1)}) conditional(s32[]{:T(128)} %clamp.43, f32[1,256,768]{2,1,0:T(8,128)S(1)} %fusion.1185, (f32[1,1,256]{2,1,0:T(1,128)}, f32[1,256,768]{2,1,0:T(8,128)S(1)}, f32[1,768]{1,0:T(1,128)S(1)}, f32[1,768]{1,0:T(1,128)S(1)}, bf16[768,3072]{1,0:T(8,128)(2,1)}, ...), branch_computations={%region_9.10_spmd, %region_10.15_spmd, %region_15.18_spmd} | conditional | flops 2470183168 | bytes 35918552 | solution.py:285
  135.2 4.6 convolution_add_fusion.3
  160.3 4.9 collective-permute-done.2
  165.9 27.0 %conditional.16 = (f32[1,256,768]{2,1,0:T(8,128)S(1)}) conditional(s32[]{:T(128)} %clamp.44, f32[1,256,768]{2,1,0:T(8,128)S(1)} %fusion.1186, (f32[1,1,256]{2,1,0:T(1,128)}, f32[1,256,768]{2,1,0:T(8,128)S(1)}, f32[1,768]{1,0:T(1,128)S(1)}, f32[1,768]{1,0:T(1,128)S(1)}, bf16[768,3072]{1,0:T(8,128)(2,1)}, ...), branch_computations={%region_18.19_spmd, %region_19.24_spmd, %region_24.27_spmd} | conditional | flops 2470183168 | bytes 35918552 | solution.py:285
  171.5 4.6 convolution_add_fusion.6
  201.4 27.4 %conditional.17 = (f32[1,256,768]{2,1,0:T(8,128)S(1)}) conditional(s32[]{:T(128)} %clamp.45, f32[1,256,768]{2,1,0:T(8,128)S(1)} %fusion.1187, (f32[1,1,256]{2,1,0:T(1,128)}, f32[1,256,768]{2,1,0:T(8,128)S(1)}, f32[1,768]{1,0:T(1,128)S(1)}, f32[1,768]{1,0:T(1,128)S(1)}, bf16[768,3072]{1,0:T(8,128)(2,1)}, ...), branch_computations={%region_27.28_spmd, %region_28.33_spmd, %region_33.36_spmd} | conditional | flops 2470183168 | bytes 35918552 | solution.py:285
  207.1 4.6 convolution_add_fusion.9
  236.4 4.6 conditional.18
  242.8 16.5 %collective-permute-start.5 = (bf16[1,256,768]{2,1,0:T(8,128)(2,1)S(1)}, bf16[1,256,768]{2,1,0:T(8,128)(2,1)S(1)}, u32[]{:S(2)}, u32[]{:S(2)}) collective-permute-start(bf16[1,256,768]{2,1,0:T(8,128)(2,1)S(1)} %get-tuple-element.1030), channel_id=1, source_target_pairs={{0,8},{8,16},{16,24},{1,9},{9,17},{17,25},{2,10},{10,18},{18,26},{... | collective-permute-start | bytes 1179656 | tf_op jit(solution)/shard_map/ppermute | solution.py:13
  270.2 13.6 %collective-permute-start.6 = (bf16[1,256,768]{2,1,0:T(8,128)(2,1)S(1)}, bf16[1,256,768]{2,1,0:T(8,128)(2,1)S(1)}, u32[]{:S(2)}, u32[]{:S(2)}) collective-permute-start(bf16[1,256,768]{2,1,0:T(8,128)(2,1)S(1)} %get-tuple-element.1028), channel_id=1, source_target_pairs={{0,8},{8,16},{16,24},{1,9},{9,17},{17,25},{2,10},{10,18},{18,26},{... | collective-permute-start | bytes 1179656 | tf_op jit(solution)/shard_map/ppermute | solution.py:13
  284.0 5.0 collective-permute-done.6
  291.2 14.8 %conditional.21 = (f32[1,256,768]{2,1,0:T(8,128)}, f32[768]{0:T(1024)}, f32[768]{0:T(1024)}, f32[768,3072]{1,0:T(8,128)}, f32[3072]{0:T(1024)}, /*index=5*/f32[768]{0:T(1024)}, f32[3072,768]{1,0:T(8,128)}) conditional(s32[]{:T(128)} %clamp.49, f32[1,256,768]{2,1,0:T(8,128)} %fusion.1180, (f32[1,256,768]{2,1,0:T(8,128)S(1)}, ...), branch_computations={%region_63.64_spmd, %region_64.78_spmd, %region_78.0_spmd} | conditional | flops 6111556096 | bytes 143189248 | solution.py:309
  297.8 4.9 broadcast.3421
  312.3 29.7 %collective-permute-done.7 = bf16[1,256,768]{2,1,0:T(8,128)(2,1)S(1)} collective-permute-done((bf16[1,256,768]{2,1,0:T(8,128)(2,1)S(1)}, bf16[1,256,768]{2,1,0:T(8,128)(2,1)S(1)}, u32[]{:S(2)}, u32[]{:S(2)}) %collective-permute-start.7) | collective-permute-done | bytes 393248 | tf_op jit(solution)/shard_map/ppermute | solution.py:13
  343.1 15.0 %conditional.22 = (f32[1,256,768]{2,1,0:T(8,128)S(1)}, f32[768]{0:T(1024)}, f32[768]{0:T(1024)}, f32[768,3072]{1,0:T(8,128)}, f32[3072]{0:T(1024)}, /*index=5*/f32[768]{0:T(1024)}, f32[3072,768]{1,0:T(8,128)}) conditional(s32[]{:T(128)} %clamp.50, f32[1,256,768]{2,1,0:T(8,128)S(1)} %fusion.1179, ...), branch_computations={%region_87.88_spmd, %region_88.102_spmd, %region_102.0_spmd} | conditional | flops 6111556096 | bytes 143197504 | solution.py:309
  349.8 4.8 broadcast.3478
  363.8 7.3 collective-permute-done.8
  372.2 14.8 %conditional.23 = (f32[1,256,768]{2,1,0:T(8,128)S(1)}, f32[768]{0:T(1024)}, f32[768]{0:T(1024)}, f32[768,3072]{1,0:T(8,128)}, f32[3072]{0:T(1024)}, /*index=5*/f32[768]{0:T(1024)}, f32[3072,768]{1,0:T(8,128)}) conditional(s32[]{:T(128)} %clamp.51, f32[1,256,768]{2,1,0:T(8,128)S(1)} %fusion.1178, ...), branch_computations={%region_111.112_spmd, %region_112.126_spmd, %region_126.0_spmd} | conditional | flops 6111556096 | bytes 143197504 | solution.py:309
  378.8 4.9 broadcast.3535
  392.7 116.8 %collective-permute-done.9 = bf16[1,256,768]{2,1,0:T(8,128)(2,1)S(1)} collective-permute-done((bf16[1,256,768]{2,1,0:T(8,128)(2,1)S(1)}, bf16[1,256,768]{2,1,0:T(8,128)(2,1)S(1)}, u32[]{:S(2)}, u32[]{:S(2)}) %collective-permute-start.9) | collective-permute-done | bytes 393248 | tf_op jit(solution)/shard_map/ppermute | solution.py:13
  510.6 68.1 %conditional.24 = (f32[1,256,768]{2,1,0:T(8,128)S(1)}, f32[768]{0:T(1024)}, f32[768]{0:T(1024)}, f32[768,3072]{1,0:T(8,128)}, f32[3072]{0:T(1024)}, /*index=5*/f32[768]{0:T(1024)}, f32[3072,768]{1,0:T(8,128)}) conditional(s32[]{:T(128)} %clamp.52, f32[1,256,768]{2,1,0:T(8,128)S(1)} %fusion.1177, ...), branch_computations={%region_135.136_spmd, %region_136.150_spmd, %region_150.0_spmd} | conditional | flops 6111556096 | bytes 143197504 | solution.py:309
  516.3 4.6 convolution_add_fusion.27
  562.4 8.7 pad_maximum_fusion.48
  584.4 5.9 collective-permute-done.10
  590.4 68.1 %conditional.25 = (f32[1,256,768]{2,1,0:T(8,128)S(1)}, f32[768]{0:T(1024)}, f32[768]{0:T(1024)}, f32[768,3072]{1,0:T(8,128)}, f32[3072]{0:T(1024)}, /*index=5*/f32[768]{0:T(1024)}, f32[3072,768]{1,0:T(8,128)}) conditional(s32[]{:T(128)} %clamp.53, f32[1,256,768]{2,1,0:T(8,128)S(1)} %select_convert_fusion.2, ...), branch_computations={%region_159.160_spmd, %region_160.174_spmd, %region_174.0_spmd} | conditional | flops 6111556096 | bytes 143197504 | solution.py:309
  596.0 4.6 convolution_add_fusion.29
  642.3 8.7 pad_maximum_fusion.64
  664.2 5.9 collective-permute-done.11
  670.2 68.6 %conditional.26 = (f32[1,256,768]{2,1,0:T(8,128)S(1)}, f32[768]{0:T(1024)}, f32[768]{0:T(1024)}, f32[768,3072]{1,0:T(8,128)}, f32[3072]{0:T(1024)}, /*index=5*/f32[768]{0:T(1024)}, f32[3072,768]{1,0:T(8,128)}) conditional(s32[]{:T(128)} %clamp.54, f32[1,256,768]{2,1,0:T(8,128)S(1)} %select_convert_fusion.1, ...), branch_computations={%region_183.184_spmd, %region_184.198_spmd, %region_198.0_spmd} | conditional | flops 6111556096 | bytes 143197504 | solution.py:309
  675.9 4.6 convolution_add_fusion.31
  722.3 8.8 pad_maximum_fusion.80
  742.7 7.7 collective-permute-done.12
  750.4 71.5 %conditional.27 = (f32[1,256,768]{2,1,0:T(8,128)S(1)}, f32[768]{0:T(1024)}, f32[768]{0:T(1024)}, f32[768,3072]{1,0:T(8,128)}, f32[3072]{0:T(1024)}, /*index=5*/f32[768]{0:T(1024)}, f32[3072,768]{1,0:T(8,128)}) conditional(s32[]{:T(128)} %clamp.55, f32[1,256,768]{2,1,0:T(8,128)S(1)} %select_convert_fusion, ...), branch_computations={%region_207.208_spmd, %region_208.222_spmd, %region_222.0_spmd} | conditional | flops 6111556096 | bytes 143197504 | solution.py:309
  756.1 4.6 convolution_add_fusion.33
  768.3 4.6 fusion.1259
  802.5 8.7 pad_maximum_fusion.96
  822.0 23.5 %add_convert_fusion.63 = bf16[3072,768]{1,0:T(8,128)(2,1)} fusion(f32[3072,768]{1,0:T(8,128)} %get-tuple-element.924, f32[3072,768]{1,0:T(8,128)} %get-tuple-element.923, f32[3072,768]{1,0:T(8,128)} %get-tuple-element.922, f32[3072,768]{1,0:T(8,128)} %get-tuple-element.921, f32[3072,768]{1,0:T(8,128)} %get-tuple-element.920, ...), kind=kLoop, calls=%fused_computation.1687 | loop fusion | flops 16515072 | bytes 70778880 | tf_op jit(solution)/shard_map/convert_element_type | solution.py:339
  845.5 24.3 %fusion.1176 = bf16[1,768,3072]{2,1,0:T(8,128)(2,1)} fusion(f32[768,3072]{1,0:T(8,128)} %get-tuple-element.903, f32[768,3072]{1,0:T(8,128)} %get-tuple-element.902, f32[768,3072]{1,0:T(8,128)} %get-tuple-element.901, f32[768,3072]{1,0:T(8,128)} %get-tuple-element.900, f32[768,3072]{1,0:T(8,128)} %get-tuple-element.899, f32[768,3072]{1,0:T(8,128)} %get-tuple-element.897, ...), kind=kLoop, calls=%fused_computation.1689 | loop fusion | flops 16515072 | bytes 70778880 | tf_op jit(solution)/shard_map/broadcast_in_dim | solution.py:357
  878.8 186.2 %all-reduce.46.cloned.1.call-done = (bf16[1,768,3072]{2,1,0:T(8,128)(2,1)}, bf16[3072,768]{1,0:T(8,128)(2,1)}) async-done(((bf16[1,768,3072]{2,1,0:T(8,128)(2,1)}, bf16[3072,768]{1,0:T(8,128)(2,1)}), (bf16[1,768,3072]{2,1,0:T(8,128)(2,1)}, bf16[3072,768]{1,0:T(8,128)(2,1)})) %all-reduce.46.cloned.1.call-update) | async-done | bytes 9437200 | tf_op jit(solution)/shard_map/psum | solution.py:336
  1071.4 6.2 all-to-all-start.1
  1080.8 27.4 %all-reduce.42 = (bf16[1,768]{1,0:T(2,128)(2,1)S(1)}, bf16[1,768]{1,0:T(2,128)(2,1)S(1)}, bf16[1,3072]{1,0:T(2,128)(2,1)S(1)}, bf16[1,768]{1,0:T(2,128)(2,1)S(1)}) all-reduce(bf16[1,768]{1,0:T(2,128)(2,1)S(1)} %broadcast_in_dim.464, bf16[1,768]{1,0:T(2,128)(2,1)S(1)} %broadcast_in_dim.466, ...), channel_id=1, replica_groups=mesh['section'=4,'dp'=8] {'dp'}, use_global_device_ids=true, to_apply=%region_231.232 | all-reduce | flops 5376 | bytes 21504 | tf_op jit(solution)/shard_map/psum | solution.py:334
  1110.5 29.5 %all-to-all-done.1 = bf16[4,1,256,768]{3,2,1,0:T(8,128)(2,1)S(1)} async-done(((bf16[4,1,256,768]{3,2,1,0:T(8,128)(2,1)}), bf16[4,1,256,768]{3,2,1,0:T(8,128)(2,1)S(1)}, u32[]{:S(2)}, u32[]{:S(2)}) %all-to-all-start.1) | async-done | bytes 1572896 | tf_op jit(solution)/shard_map/all_to_all | solution.py:327
  1140.8 7.9 broadcast_in_dim.469
  1148.7 4.6 select_bitcast_fusion
  (707 shorter events, 402.2 us)
Async XLA Ops:
  7.2 82.7 %all-gather.3.cloned.1.call-start = ((), (), s32[]{:S(2)}) async-start(), calls=%async_computation.2 | async-start | bytes 1966080 | tf_op jit(solution)/shard_map/all_gather | solution.py:255
  7.9 115.9 %all-gather.5.cloned.1.call-start = ((), (), s32[]{:S(2)}) async-start(), calls=%async_computation.3 | async-start | bytes 1966080 | tf_op jit(solution)/shard_map/all_gather | solution.py:256
  7.9 83.0 %collective-permute-start = (bf16[1,1536,768]{2,1,0:T(8,128)(2,1)}, bf16[1,1536,768]{2,1,0:T(8,128)(2,1)S(1)}, u32[]{:S(2)}, u32[]{:S(2)}) collective-permute-start(bf16[1,1536,768]{2,1,0:T(8,128)(2,1)} %param.61), channel_id=1, source_target_pairs={{0,8},{8,16},{16,24},{1,9},{9,17},{17,25},{2,10},{10,18},{18,26},{... | collective-permute-start | bytes 7077896 | tf_op jit(solution)/shard_map/ppermute | solution.py:13
  13.0 1052.1 %all-reduce.46.cloned.1.call-start = ((), (), s32[]{:S(2)}) async-start(), calls=%async_computation.4 | async-start | bytes 18874368 | tf_op jit(solution)/shard_map/psum | solution.py:336
  95.2 8.7 copy-start.272
  120.2 8.1 collective-permute-start.1
  157.7 7.5 collective-permute-start.2
  193.9 6.8 collective-permute-start.3
  229.7 6.6 collective-permute-start.4
  242.8 21.8 %collective-permute-start.5 = (bf16[1,256,768]{2,1,0:T(8,128)(2,1)S(1)}, bf16[1,256,768]{2,1,0:T(8,128)(2,1)S(1)}, u32[]{:S(2)}, u32[]{:S(2)}) collective-permute-start(bf16[1,256,768]{2,1,0:T(8,128)(2,1)S(1)} %get-tuple-element.1030), channel_id=1, source_target_pairs={{0,8},{8,16},{16,24},{1,9},{9,17},{17,25},{2,10},{10,18},{18,26},{... | collective-permute-start | bytes 1179656 | tf_op jit(solution)/shard_map/ppermute | solution.py:13
  270.2 18.8 %collective-permute-start.6 = (bf16[1,256,768]{2,1,0:T(8,128)(2,1)S(1)}, bf16[1,256,768]{2,1,0:T(8,128)(2,1)S(1)}, u32[]{:S(2)}, u32[]{:S(2)}) collective-permute-start(bf16[1,256,768]{2,1,0:T(8,128)(2,1)S(1)} %get-tuple-element.1028), channel_id=1, source_target_pairs={{0,8},{8,16},{16,24},{1,9},{9,17},{17,25},{2,10},{10,18},{18,26},{... | collective-permute-start | bytes 1179656 | tf_op jit(solution)/shard_map/ppermute | solution.py:13
  309.2 32.8 %collective-permute-start.7 = (bf16[1,256,768]{2,1,0:T(8,128)(2,1)S(1)}, bf16[1,256,768]{2,1,0:T(8,128)(2,1)S(1)}, u32[]{:S(2)}, u32[]{:S(2)}) collective-permute-start(bf16[1,256,768]{2,1,0:T(8,128)(2,1)S(1)} %get-tuple-element.1026), channel_id=1, source_target_pairs={{8,0},{16,8},{24,16},{9,1},{17,9},{25,17},{10,2},{18,10},{26,18},{... | collective-permute-start | bytes 1179656 | tf_op jit(solution)/shard_map/ppermute | solution.py:13
  358.1 14.0 %copy-start.4 = (f32[1,256,768]{2,1,0:T(8,128)S(1)}, f32[1,256,768]{2,1,0:T(8,128)}, u32[]{:S(2)}) copy-start(f32[1,256,768]{2,1,0:T(8,128)} %get-tuple-element.1372) | copy-start | bytes 2359300
  358.1 14.0 %copy-start.244 = (f32[1,3,256]{2,1,0:T(4,128)S(1)}, f32[1,3,256]{2,1,0:T(4,128)}, u32[]{:S(2)}) copy-start(f32[1,3,256]{2,1,0:T(4,128)} %get-tuple-element.1379) | copy-start | bytes 9220
  360.1 11.0 collective-permute-start.8
  387.0 123.6 %copy-start.3 = (f32[1,256,768]{2,1,0:T(8,128)S(1)}, f32[1,256,768]{2,1,0:T(8,128)}, u32[]{:S(2)}) copy-start(f32[1,256,768]{2,1,0:T(8,128)} %get-tuple-element.1371) | copy-start | bytes 2359300
  387.0 123.6 %copy-start.243 = (f32[1,3,256]{2,1,0:T(4,128)S(1)}, f32[1,3,256]{2,1,0:T(4,128)}, u32[]{:S(2)}) copy-start(f32[1,3,256]{2,1,0:T(4,128)} %get-tuple-element.1378) | copy-start | bytes 9220
  389.0 120.6 %collective-permute-start.9 = (bf16[1,256,768]{2,1,0:T(8,128)(2,1)S(1)}, bf16[1,256,768]{2,1,0:T(8,128)(2,1)S(1)}, u32[]{:S(2)}, u32[]{:S(2)}) collective-permute-start(bf16[1,256,768]{2,1,0:T(8,128)(2,1)S(1)} %get-tuple-element.1022), channel_id=1, source_target_pairs={{8,0},{16,8},{24,16},{9,1},{17,9},{25,17},{10,2},{18,10},{26,18},{... | collective-permute-start | bytes 1179656 | tf_op jit(solution)/shard_map/ppermute | solution.py:13
  510.6 10.3 copy-start.152
  511.3 9.6 copy-start.177
  511.6 9.3 copy-start.259
  511.6 9.3 copy-start.231
  578.7 11.7 %copy-start.2 = (f32[1,256,768]{2,1,0:T(8,128)S(1)}, f32[1,256,768]{2,1,0:T(8,128)}, u32[]{:S(2)}) copy-start(f32[1,256,768]{2,1,0:T(8,128)} %get-tuple-element.1370) | copy-start | bytes 2359300
  578.7 11.7 %copy-start.242 = (f32[1,3,256]{2,1,0:T(4,128)S(1)}, f32[1,3,256]{2,1,0:T(4,128)}, u32[]{:S(2)}) copy-start(f32[1,3,256]{2,1,0:T(4,128)} %get-tuple-element.1377) | copy-start | bytes 9220
  580.7 9.7 collective-permute-start.10
  590.4 10.2 copy-start.162
  591.1 9.5 copy-start.179
  591.3 9.3 copy-start.261
  591.3 9.3 copy-start.233
  658.5 11.7 %copy-start.1 = (f32[1,256,768]{2,1,0:T(8,128)S(1)}, f32[1,256,768]{2,1,0:T(8,128)}, u32[]{:S(2)}) copy-start(f32[1,256,768]{2,1,0:T(8,128)} %get-tuple-element.1369) | copy-start | bytes 2359300
  658.5 11.7 %copy-start.241 = (f32[1,3,256]{2,1,0:T(4,128)S(1)}, f32[1,3,256]{2,1,0:T(4,128)}, u32[]{:S(2)}) copy-start(f32[1,3,256]{2,1,0:T(4,128)} %get-tuple-element.1376) | copy-start | bytes 9220
  660.5 9.7 collective-permute-start.11
  670.2 10.3 copy-start.165
  670.9 9.6 copy-start.181
  671.2 9.4 copy-start.263
  671.2 9.3 copy-start.235
  671.9 8.7 copy-start.129
  738.8 11.7 %copy-start = (f32[1,256,768]{2,1,0:T(8,128)S(1)}, f32[1,256,768]{2,1,0:T(8,128)}, u32[]{:S(2)}) copy-start(f32[1,256,768]{2,1,0:T(8,128)} %get-tuple-element.1368) | copy-start | bytes 2359300
  738.8 11.7 %copy-start.240 = (f32[1,3,256]{2,1,0:T(4,128)S(1)}, f32[1,3,256]{2,1,0:T(4,128)}, u32[]{:S(2)}) copy-start(f32[1,3,256]{2,1,0:T(4,128)} %get-tuple-element.1375) | copy-start | bytes 9220
  740.7 9.7 collective-permute-start.12
  750.5 10.2 copy-start.168
  751.2 9.5 copy-start.183
  751.4 9.3 copy-start.265
  751.4 9.3 copy-start.237
  752.0 8.7 copy-start.131
  875.2 196.2 %all-to-all-start = ((bf16[4,1,256,768]{3,2,1,0:T(8,128)(2,1)}), bf16[4,1,256,768]{3,2,1,0:T(8,128)(2,1)S(1)}, u32[]{:S(2)}, u32[]{:S(2)}) async-start(bf16[4,1,256,768]{3,2,1,0:T(8,128)(2,1)} %bitcast_dynamic-update-slice_fusion.14), calls=%async_computation | async-start | bytes 3145728 | tf_op jit(solution)/shard_map/all_to_all | solution.py:326
  1068.3 80.4 %collective-permute-start.13 = (bf16[1536,768]{1,0:T(8,128)(2,1)}, bf16[1536,768]{1,0:T(8,128)(2,1)}, u32[]{:S(2)}, u32[]{:S(2)}) collective-permute-start(bf16[1536,768]{1,0:T(8,128)(2,1)} %slice.1121), channel_id=1, source_target_pairs={{8,0},{16,8},{24,16},{9,1},{17,9},{25,17},{10,2},{18,10},{26,18},{... | collective-permute-start | bytes 7077896 | tf_op jit(solution)/shard_map/ppermute | solution.py:13
  1071.4 68.6 %all-to-all-start.1 = ((bf16[4,1,256,768]{3,2,1,0:T(8,128)(2,1)}), bf16[4,1,256,768]{3,2,1,0:T(8,128)(2,1)S(1)}, u32[]{:S(2)}, u32[]{:S(2)}) async-start(bf16[4,1,256,768]{3,2,1,0:T(8,128)(2,1)} %bitcast_dynamic-update-slice_fusion), calls=%async_computation.1 | async-start | bytes 3145728 | tf_op jit(solution)/shard_map/all_to_all | solution.py:327
  (137 other events, 327.3 us)
Sparse Core Ops, SparseCore 0:
  9.8 46.5 all-gather.2
  58.3 35.5 all-gather.4
  869.9 195.0 all-reduce.45
where the time goes:
time: 1170 us; the launch traced here: 1160 us
  waiting for transfers between devices  412 us (35%)
  other arithmetic  213 us (18%)
  local copies, waits for them, and re-layouts  156 us (13%)
  matrix products  146 us (12%)
  blocking collectives  97.3 us (8%)
  loops' own time  60.2 us (5%)
  starting transfers between devices  59.1 us (5%)
  between operations  16 us (1%)
    ppermute x14, waiting for transfers between devices, shifted(): return lax.ppermute(x, axis, pairs)  196 us
    psum x1, waiting for transfers between devices, on_device(): lax.psum(grad_matrix.astype(jnp.bfloat16), 'dp').astype(jnp.float32)  186 us
    all_gather x1, blocking collectives, on_device(): lax.all_gather(table_local, 'section', axis=0, tiled=True)  69.9 us
    another operation x25, local copies, waits for them, and re-layouts  53.7 us
    ppermute x14, starting transfers between devices, shifted(): return lax.ppermute(x, axis, pairs)  49.2 us
    dot_general x8, matrix products, mixer_core(): jnp.dot(normed_low, matrix[:, :3 * model_width], preferred_element_type=j...  36.6 us
    concatenate x4, other arithmetic, mixer_backward(): jnp.concatenate([grad_in_w, grad_out_w], axis=1)  35 us
    broadcast_in_dim x2, other arithmetic, on_device(): sum_matrix[None]  32.2 us
  transfers between devices with their start and end apart: 19, of which 14 were waited for; matrix products, arithmetic and copies ran while one was open for 6% of the time, Pallas kernels for 0%

commit v1 on v0

v1 whole, which is shorter than its diff:
```python
import functools

import jax
import jax.numpy as jnp
from jax import lax
from jax.experimental import pallas as pl
from jax.experimental.pallas import tpu as pltpu
from jax.sharding import PartitionSpec as P

HEADS = 12
HEAD_DIM = 64
GROUP = 256
EPS = 1e-06
MESH = pl.DeviceIdType.MESH
BF = jnp.bfloat16
F32 = jnp.float32
HI = lax.Precision.HIGHEST
LAG_SIB, LAG_ONE, LAG_TWO, LAG_END = 1, 2, 4, 6


def nn(a, b, precision=None):
    return lax.dot_general(a, b, (((1,), (0,)), ((), ())), precision=precision, preferred_element_type=F32)


def nt(a, b, precision=None):
    return lax.dot_general(a, b, (((1,), (1,)), ((), ())), precision=precision, preferred_element_type=F32)


def tn(a, b, precision=None):
    return lax.dot_general(a, b, (((0,), (0,)), ((), ())), precision=precision, preferred_element_type=F32)


def normalise(x):
    centered = x - jnp.mean(x, axis=-1, keepdims=True)
    scale = lax.rsqrt(jnp.mean(centered * centered, axis=-1, keepdims=True) + EPS)
    return centered * scale, scale


def relay(
    n_sec, lines, tokens, width, ff,
    patches, cot, tab, wm, wd, gain, bias, bm, sv,
    o_out, o_ig, o_w, o_d, o_small,
    hin, gin, act, big1, big2, big3, wv, dv, cs, tabs, hout, gout, perm, bqk, freq,
    mine, zin, pin, sib, tmp, sg, sg_sib, sg_one, sg_two,
    w_sem, hin_r, gin_r, tab_r, hop_s, gop_s, ini_s, wd_s, wd_r, out_r, ig_r,
    sib_s, sib_r, low_s, mine_r, za_s, zin_r, pb_s, pin_r, fin_l, fin_s, fin_r, sg_s, sg_r,
):
    s = lax.axis_index("section")
    d = lax.axis_index("dp")
    core = lax.rem(d, 2)
    other = d + 1 - 2 * core
    even = lax.rem(s, 2) == 0
    odd = lax.rem(s, 2) == 1
    last = n_sec - 1
    half = tokens // 2
    n_main = (width // 256) * (ff // width)
    n_low = (ff // 2) // 256
    n_chunk = n_main + n_low
    score_scale = HEAD_DIM ** (-0.5)

    def to_section(target):
        return {"section": target}

    def to_dp(target):
        return {"dp": target}

    def remote(src, dst, send, recv, device):
        return pltpu.make_async_remote_copy(
            src_ref=src, dst_ref=dst, send_sem=send, recv_sem=recv, device_id=device, device_id_type=MESH
        )

    spots = []
    for stride in lines:
        pos = lax.rem(d // stride, 4)
        near = d + (1 - 2 * lax.rem(pos, 2)) * stride
        across = d + (3 - 2 * pos) * stride
        inner = (pos == 1) | (pos == 2)
        outer = (pos == 0) | (pos == 3)
        spots.append((near, across, inner, outer))

    barrier = pltpu.get_barrier_semaphore()
    for step in range(1, n_sec):
        pl.semaphore_signal(barrier, inc=1, device_id=to_section(lax.rem(s + step, n_sec)), device_id_type=MESH)
    pl.semaphore_signal(barrier, inc=1, device_id=to_dp(other), device_id_type=MESH)
    for near, across, inner, outer in spots:
        pl.semaphore_signal(barrier, inc=1, device_id=to_dp(near), device_id_type=MESH)

        @pl.when(inner)
        def _():
            pl.semaphore_signal(barrier, inc=1, device_id=to_dp(across), device_id_type=MESH)

    load_w = pltpu.make_async_copy(wm.at[0], wv, w_sem.at[0])
    load_d = pltpu.make_async_copy(wd.at[0], dv.at[pl.ds(ff // 2, ff // 2)], w_sem.at[1])
    load_w.start()

    @pl.when(odd)
    def _():
        load_d.start()

    peers = n_sec + len(spots)
    for near, across, inner, outer in spots:
        peers = peers + jnp.where(inner, 1, 0)
    pl.semaphore_wait(barrier, peers)

    tab_sends = []
    for step in range(1, n_sec):
        tab_sends.append(
            remote(tab.at[0], tabs.at[s], ini_s.at[step - 1], tab_r.at[s], to_section(lax.rem(s + step, n_sec)))
        )
    for send in tab_sends:
        send.start()
    tab_own = pltpu.make_async_copy(tab.at[0], tabs.at[s], tab_r.at[s])
    tab_own.start()
    patch_send = remote(patches.at[0], hin.at[s], ini_s.at[n_sec], hin_r.at[s], to_section(0))
    patch_own = pltpu.make_async_copy(patches.at[0], hin.at[0], hin_r.at[0])
    cot_send = remote(cot.at[0], gin.at[s], ini_s.at[n_sec + 1], gin_r.at[s], to_section(last))
    cot_own = pltpu.make_async_copy(cot.at[0], gin.at[last], gin_r.at[last])

    @pl.when(s == 0)
    def _():
        patch_own.start()

    @pl.when(s != 0)
    def _():
        patch_send.start()

    @pl.when(s == last)
    def _():
        cot_own.start()

    down_half = (ff // 2) // 2
    mine_rows = pl.ds(pl.multiple_of(core * down_half, down_half), down_half)
    their_rows = pl.ds(pl.multiple_of((1 - core) * down_half, down_half), down_half)
    down_send = remote(
        wd.at[0, mine_rows], dv.at[mine_rows], wd_s.at[0], wd_r.at[0], to_section(lax.rem(s + 1, n_sec))
    )
    down_pass = remote(dv.at[mine_rows], dv.at[mine_rows], wd_s.at[1], wd_r.at[1], to_dp(other))
    down_pass_in = remote(dv.at[their_rows], dv.at[their_rows], wd_s.at[1], wd_r.at[1], to_dp(other))

    @pl.when(even)
    def _():
        down_send.start()

    sg[...] = jnp.zeros_like(sg)
    load_w.wait()

    @pl.when(even)
    def _():
        old = lax.broadcasted_iota(jnp.int32, (GROUP, GROUP), 0)
        new = lax.broadcasted_iota(jnp.int32, (GROUP, GROUP), 1)
        source = ((new & 127) >> 5) * 64 + (new >> 7) * 32 + (new & 31)
        perm[...] = jnp.where(old == source, 1.0, 0.0).astype(BF)
        table = perm[...]
        for block in range(2 * width // GROUP):
            columns = slice(block * GROUP, (block + 1) * GROUP)
            wv[:, columns] = nn(wv[:, columns], table).astype(BF)
            row = jnp.broadcast_to(bm[:, columns], (8, GROUP))
            bqk[:, columns] = nn(row, table.astype(F32), HI)
        freq[...] = jnp.zeros_like(freq)
        freq[0:1, :] = sv[:, : width // 2]
        freq[1:2, :] = sv[:, width // 2 :]

    lane = lax.broadcasted_iota(jnp.int32, (1, GROUP), 1)
    q_masks = [((lane & 127) >> 5) == e for e in range(4)]
    v_masks = [(lane >> 6) == e for e in range(4)]
    zero_low = jnp.zeros((), BF)

    def count_of(i):
        return tabs[i, 2:3, 0:1]

    def row_mask(i):
        ids = lax.broadcasted_iota(jnp.int32, (tokens, 1), 0).astype(F32)
        return jnp.where(ids < count_of(i), 1.0, 0.0)

    def key_mask(i):
        ids = lax.broadcasted_iota(jnp.int32, (1, tokens), 1).astype(F32)
        return ids < count_of(i)

    n_group = width // GROUP
    pairs = width // 2 // n_group

    def attention_forward(i, slot):
        x = hin[i].astype(F32)
        xhat, _ = normalise(x)
        a = (xhat * gain[...] + bias[...]).astype(BF)
        act[i] = a
        angle = nn(jnp.transpose(tabs[i]), freq[...], HI)
        cs[i, 0] = jnp.cos(angle)
        cs[i, 1] = jnp.sin(angle)
        keys_on = key_mask(i)
        for g in range(n_group):
            cosine = cs[i, 0, :, g * pairs : (g + 1) * pairs]
            sine = cs[i, 1, :, g * pairs : (g + 1) * pairs]
            turned = []
            for which in range(2):
                lo = which * width + g * GROUP
                t = nn(a, wv[:, lo : lo + GROUP]) + bqk[0:1, lo : lo + GROUP]
                t1, t2 = t[:, :128], t[:, 128:]
                r = jnp.concatenate([t1 * cosine - t2 * sine, t1 * sine + t2 * cosine], axis=1).astype(BF)
                big1[i, :, lo : lo + GROUP] = r
                turned.append(r)
            lo = 2 * width + g * GROUP
            value = (nn(a, wv[:, lo : lo + GROUP]) + bm[:, lo : lo + GROUP]).astype(BF)
            big1[i, :, lo : lo + GROUP] = value
            query, key = turned
            context = jnp.zeros((tokens, GROUP), F32)
            for e in range(4):
                scores = nt(jnp.where(q_masks[e], query, zero_low), key) * score_scale
                scores = jnp.where(keys_on, scores, -1e30)
                top = jnp.max(scores, axis=-1, keepdims=True)
                p = jnp.exp(scores - top)
                p = (p * (1.0 / jnp.sum(p, axis=-1, keepdims=True))).astype(BF)
                big2[i, :, (4 * g + e) * tokens : (4 * g + e + 1) * tokens] = p
                context = jnp.where(v_masks[e], nn(p, value), context)
            lo = 3 * width + g * GROUP
            big1[i, :, lo : lo + GROUP] = context.astype(BF)
        branch = nn(big1[i, :, 3 * width :], wv[:, 3 * width :]) + bm[:, 3 * width :]
        hout[slot] = (x + row_mask(i) * branch).astype(BF)

    def norm_backward(i, g_up, gact):
        xhat, scale = normalise(hin[i].astype(F32))
        sg[0:1, :] += jnp.sum(gact * xhat, axis=0, keepdims=True)
        sg[1:2, :] += jnp.sum(gact, axis=0, keepdims=True)
        gn = gact * gain[...]
        inside = gn - jnp.mean(gn, axis=-1, keepdims=True) - xhat * jnp.mean(gn * xhat, axis=-1, keepdims=True)
        return g_up + scale * inside

    def attention_backward(i, slot):
        g_up = gin[i].astype(F32)
        gb = row_mask(i) * g_up
        sg[6:7, :] += jnp.sum(gb, axis=0, keepdims=True)
        low = gb.astype(BF)
        dctx_all = nt(low, wv[:, 3 * width :]).astype(BF)
        for g in range(n_group):
            qlo, klo, vlo = g * GROUP, width + g * GROUP, 2 * width + g * GROUP
            query = big1[i, :, qlo : qlo + GROUP]
            key = big1[i, :, klo : klo + GROUP]
            value = big1[i, :, vlo : vlo + GROUP]
            dctx = dctx_all[:, g * GROUP : (g + 1) * GROUP]
            dq = jnp.zeros((tokens, GROUP), F32)
            dk = jnp.zeros((tokens, GROUP), F32)
            dval = jnp.zeros((tokens, GROUP), F32)
            for e in range(4):
                d_e = jnp.where(v_masks[e], dctx, zero_low)
                q_e = jnp.where(q_masks[e], query, zero_low)
                gw = nt(d_e, value)
                p_low = big2[i, :, (4 * g + e) * tokens : (4 * g + e + 1) * tokens]
                p = p_low.astype(F32)
                pg = p * gw
                gs = (pg - p * jnp.sum(pg, axis=-1, keepdims=True)).astype(BF)
                dq = jnp.where(q_masks[e], nn(gs, key), dq)
                dk = dk + tn(gs, q_e)
                dval = dval + tn(p_low, d_e)
            cosine = cs[i, 0, :, g * pairs : (g + 1) * pairs]
            sine = cs[i, 1, :, g * pairs : (g + 1) * pairs]
            turn = jnp.zeros((tokens, pairs), F32)
            for lo, grad, held in ((qlo, dq, query), (klo, dk, key)):
                g1, g2 = grad[:, :128] * score_scale, grad[:, 128:] * score_scale
                r = held.astype(F32)
                turn = turn + g2 * r[:, :128] - g1 * r[:, 128:]
                raw = jnp.concatenate([g1 * cosine + g2 * sine, g2 * cosine - g1 * sine], axis=1).astype(BF)
                big3[i, :, lo : lo + GROUP] = raw
                row = 3 if lo < width else 4
                at = g * GROUP
                sg[row : row + 1, at : at + GROUP] += jnp.sum(raw.astype(F32), axis=0, keepdims=True)
            raw = dval.astype(BF)
            big3[i, :, vlo : vlo + GROUP] = raw
            sg[5:6, g * GROUP : (g + 1) * GROUP] += jnp.sum(raw.astype(F32), axis=0, keepdims=True)
            sums = nn(tabs[i], turn, HI)
            at = g * pairs
            sg[2:3, at : at + pairs] += sums[0:1]
            at = width // 2 + g * pairs
            sg[2:3, at : at + pairs] += sums[1:2]
        gact = nt(big3[i, :, : 3 * width], wv[:, : 3 * width])
        gout[slot] = norm_backward(i, g_up, gact).astype(BF)
        gin[i] = low

    piece = 512

    def dense_forward(i, slot):
        x = hin[i].astype(F32)
        xhat, _ = normalise(x)
        a = (xhat * gain[...] + bias[...]).astype(BF)
        act[i] = a
        for k in range(ff // piece):
            lo = k * piece
            pre = nn(a, wv[:, lo : lo + piece]) + bm[:, lo : lo + piece]
            cdf = 0.5 + 0.5 * lax.erf(pre * (0.5**0.5))
            big1[i, :, lo : lo + piece] = (pre * cdf).astype(BF)
            pdf = jnp.exp(-0.5 * (pre * pre)) * 0.3989422804014327
            big2[i, :, lo : lo + piece] = (cdf + pre * pdf).astype(BF)

        @pl.when(i == 0)
        def _():
            load_d.wait()
            down_send.wait_recv()
            down_pass.start()
            down_pass_in.wait_recv()

        branch = nn(big1[i], dv[...]) + sv[...]
        hout[slot] = (x + row_mask(i) * branch).astype(BF)

    def dense_backward(i, slot):
        g_up = gin[i].astype(F32)
        gb = row_mask(i) * g_up
        sg[2:3, :] += jnp.sum(gb, axis=0, keepdims=True)
        low = gb.astype(BF)
        for k in range(ff // width):
            for m in range(width // GROUP):
                lo = k * width + m * GROUP
                gh = nt(low, dv[lo : lo + GROUP, :])
                gpre = (gh * big2[i, :, lo : lo + GROUP].astype(F32)).astype(BF)
                big3[i, :, lo : lo + GROUP] = gpre
                at = m * GROUP
                sg[3 + k : 4 + k, at : at + GROUP] += jnp.sum(gpre.astype(F32), axis=0, keepdims=True)
        gact = nt(big3[i], wv[...])
        gout[slot] = norm_backward(i, g_up, gact).astype(BF)
        gin[i] = low

    def hop_send(i, slot):
        return remote(hout.at[slot], hin.at[i], hop_s.at[i], hin_r.at[i], to_section(lax.rem(s + 1, n_sec)))

    def result_send(i, slot):
        return remote(hout.at[slot], o_out.at[0], hop_s.at[i], out_r, to_section(i))

    def back_send(i, slot):
        return remote(gout.at[slot], gin.at[i], gop_s.at[i], gin_r.at[i], to_section(lax.rem(s + last, n_sec)))

    def input_send(i, slot):
        return remote(gout.at[slot], o_ig.at[0], gop_s.at[i], ig_r, to_section(i))

    def forward(i):
        slot = lax.rem(i, 2)

        @pl.when(i >= 2)
        def _():
            hop_send(i - 2, slot).wait_send()

        hop_send(i, slot).wait_recv()
        tab_own_like = pltpu.make_async_copy(tab.at[0], tabs.at[i], tab_r.at[i])
        tab_own_like.wait()

        @pl.when(even)
        def _():
            attention_forward(i, slot)

        @pl.when(odd)
        def _():
            dense_forward(i, slot)

        @pl.when(s != last)
        def _():
            hop_send(i, slot).start()

        @pl.when((s == last) & (i != last))
        def _():
            result_send(i, slot).start()

        @pl.when((s == last) & (i == last))
        def _():
            pltpu.make_async_copy(hout.at[slot], o_out.at[0], out_r).start()

    def backward(i):
        slot = lax.rem(i, 2)

        @pl.when((i == 3) | ((i == 2) & (s != 0)))
        def _():
            back_send(i - 2, slot).wait_send()

        @pl.when((i == 2) & (s == 0))
        def _():
            pltpu.make_async_copy(gout.at[slot], o_ig.at[0], ig_r).wait()

        back_send(i, slot).wait_recv()

        @pl.when(even)
        def _():
            attention_backward(i, slot)

        @pl.when(odd)
        def _():
            dense_backward(i, slot)

        @pl.when(s != 0)
        def _():
            back_send(i, slot).start()

        @pl.when((s == 0) & (i != 0))
        def _():
            input_send(i, slot).start()

        @pl.when((s == 0) & (i == 0))
        def _():
            pltpu.make_async_copy(gout.at[slot], o_ig.at[0], ig_r).start()

    def tick(j, carry):
        @pl.when(j < n_sec)
        def _():
            forward(j)

        @pl.when((s != last) & (((s == 0) & (j == 2)) | ((s != 0) & (j == 0))))
        def _():
            cot_send.start()

        b = j - (last - s)

        @pl.when((b >= 0) & (b < n_sec))
        def _():
            backward(b)

        return carry

    lax.fori_loop(0, 2 * n_sec - 1, tick, 0)

    @pl.when(even)
    def _():
        back = perm[...].astype(F32)
        for block in range(2 * width // GROUP):
            row = 3 + block * GROUP // width
            lo = block * GROUP % width
            part = jnp.broadcast_to(sg[row : row + 1, lo : lo + GROUP], (8, GROUP))
            sg[row : row + 1, lo : lo + GROUP] = nt(part, back, HI)[0:1]

    my_half = pl.ds(pl.multiple_of(core * half, half), half)
    their_half = pl.ds(pl.multiple_of((1 - core) * half, half), half)
    shift = jnp.where(odd, n_low, 0)
    steps = n_chunk + n_low + len(lines) * LAG_END + 1

    def flat(ref):
        return ref.reshape(n_sec * tokens, ref.shape[-1])

    def sib_slot(c):
        return jnp.where(c < 0, n_chunk + n_low + c, c)

    def sib_copy(c):
        slot = lax.rem(c + n_low, 2)
        at = sib_slot(c)
        return remote(tmp.at[slot, their_half], sib.at[at], sib_s.at[slot], sib_r.at[at], to_dp(other))

    def low_copy(c):
        at = c + n_low
        return remote(
            sib.at[n_chunk + at], mine.at[n_main + at], low_s.at[at], mine_r.at[at], to_section(lax.rem(s + last, n_sec))
        )

    def make_block(c):
        slot = lax.rem(c + n_low, 2)

        @pl.when((even & (c >= 2)) | (odd & (c >= 2 - n_low)))
        def _():
            sib_copy(c - 2).wait_send()

        column = lax.rem(c, ff // width)
        row = c // (ff // width)
        is_main = (c >= 0) & (c < n_main)
        from_act = is_main & (odd | (column < 3))

        @pl.when(from_act)
        def _():
            rows = pl.ds(pl.multiple_of(row * 256, 256), 256)
            columns = pl.ds(pl.multiple_of(column * width, width), width)
            left = act[:, :, rows].reshape(n_sec * tokens, 256)
            right = big3[:, :, columns].reshape(n_sec * tokens, width)
            tmp[slot] = tn(left, right).astype(BF)

        @pl.when(from_act & even & (column < 2))
        def _():
            back = perm[...]
            for block in range(width // GROUP):
                at = slice(block * GROUP, (block + 1) * GROUP)
                tmp[slot, :, at] = nt(tmp[slot, :, at], back).astype(BF)

        @pl.when(jnp.logical_not(from_act))
        def _():
            down_row = jnp.where(c < 0, (c + n_low) * 256, ff // 2 + (c - n_main) * 256)
            start = jnp.where(even, 3 * width + row * 256, down_row)
            rows = pl.ds(pl.multiple_of(start, 256), 256)
            left = big1[:, :, rows].reshape(n_sec * tokens, 256)
            right = gin[...].reshape(n_sec * tokens, width)
            tmp[slot] = tn(left, right).astype(BF)

        sib_copy(c).start()

    def spot_copies(k, c):
        near, across, inner, outer = spots[k]
        to_near = remote(mine.at[c], zin.at[k, c], za_s.at[k, c], zin_r.at[k, c], to_dp(near))
        to_across = remote(zin.at[k, c], pin.at[k, c], pb_s.at[k, c], pin_r.at[k, c], to_dp(across))
        return to_near, to_across

    def result_place(c):
        return c

    def w_place(c):
        row = c // (ff // width)
        column = lax.rem(c, ff // width)
        rows = pl.ds(pl.multiple_of(row * 256 + core * half, half), half)
        columns = pl.ds(pl.multiple_of(column * width, width), width)
        return o_w.at[rows, columns]

    def d_place(c):
        rows = pl.ds(pl.multiple_of((c - n_main) * 256 + core * half, half), half)
        return o_d.at[rows, :]

    def finish_copies(c, place):
        here = pltpu.make_async_copy(mine.at[c], place, fin_l.at[c])
        there = remote(mine.at[c], place, fin_s.at[c], fin_r.at[c], to_dp(other))
        return here, there

    def finish(c):
        @pl.when(c < n_main)
        def _():
            here, there = finish_copies(c, w_place(c))
            here.start()
            there.start()

        @pl.when(c >= n_main)
        def _():
            here, there = finish_copies(c, d_place(c))
            here.start()
            there.start()

    def sum_step(t, carry):
        c = t - shift

        @pl.when((even & (c < n_main)) | (odd & (c < n_chunk)))
        def _():
            make_block(c)

        c1 = c - LAG_SIB

        @pl.when((even & (c1 >= 0) & (c1 < n_main)) | (odd & (c1 >= -n_low) & (c1 < n_chunk)))
        def _():
            slot = lax.rem(c1 + n_low, 2)
            at = sib_slot(c1)
            sib_copy(c1).wait_recv()
            total = (tmp[slot, my_half].astype(F32) + sib[at].astype(F32)).astype(BF)

            @pl.when(c1 < 0)
            def _():
                sib[at] = total
                low_copy(c1).start()

            @pl.when(c1 >= 0)
            def _():
                mine[c1] = total

        @pl.when(even & (c1 >= n_main) & (c1 < n_chunk))
        def _():
            low_copy(c1 - n_chunk).wait_recv()

        for k in range(len(lines)):
            near, across, inner, outer = spots[k]
            base = LAG_SIB + k * LAG_END
            c0 = c - base

            @pl.when(outer & (c0 >= 0) & (c0 < n_chunk))
            def _():
                to_near, _ = spot_copies(k, c0)
                to_near.start()

            c2 = c - base - LAG_ONE

            @pl.when(inner & (c2 >= 0) & (c2 < n_chunk))
            def _():
                to_near, to_across = spot_copies(k, c2)
                to_near.wait_recv()
                zin[k, c2] = (mine[c2].astype(F32) + zin[k, c2].astype(F32)).astype(BF)
                to_across.start()

            c3 = c - base - LAG_TWO

            @pl.when(inner & (c3 >= 0) & (c3 < n_chunk))
            def _():
                to_near, to_across = spot_copies(k, c3)
                to_across.wait_recv()
                mine[c3] = (zin[k, c3].astype(F32) + pin[k, c3].astype(F32)).astype(BF)
                to_near.start()
                if k == len(lines) - 1:
                    finish(c3)

            c4 = c - base - LAG_END

            @pl.when(outer & (c4 >= 0) & (c4 < n_chunk))
            def _():
                to_near, _ = spot_copies(k, c4)
                to_near.wait()
                mine[c4] = zin[k, c4]
                if k == len(lines) - 1:
                    finish(c4)

        return carry

    small_sib = remote(sg, sg_sib, sg_s.at[0], sg_r.at[0], to_dp(other))
    small_sib.start()
    small_sib.wait()
    sg[...] = sg[...] + sg_sib[...]

    def small_copies(k):
        near, across, inner, outer = spots[k]
        to_near = remote(sg, sg_one.at[k], sg_s.at[1 + 2 * k], sg_r.at[1 + 2 * k], to_dp(near))
        to_across = remote(sg_one.at[k], sg_two.at[k], sg_s.at[2 + 2 * k], sg_r.at[2 + 2 * k], to_dp(across))
        return to_near, to_across

    for k in range(len(lines)):
        near, across, inner, outer = spots[k]
        to_near, to_across = small_copies(k)

        @pl.when(outer)
        def _():
            to_near.start()
            to_near.wait()
            sg[...] = sg_one[k]

        @pl.when(inner)
        def _():
            to_near.wait_recv()
            sg_one[k] = sg[...] + sg_one[k]
            to_across.start()
            to_across.wait()
            sg[...] = sg_one[k] + sg_two[k]
            to_near.start()
            to_near.wait_send()

    o_small[...] = sg[...]

    lax.fori_loop(0, steps, sum_step, 0)

    for send in tab_sends:
        send.wait_send()

    @pl.when(s != 0)
    def _():
        patch_send.wait_send()

    @pl.when(s != last)
    def _():
        cot_send.wait_send()

    @pl.when(even)
    def _():
        down_send.wait_send()
        sib_copy(n_main - 2).wait_send()
        sib_copy(n_main - 1).wait_send()

    @pl.when(odd)
    def _():
        down_pass.wait_send()
        sib_copy(n_chunk - 2).wait_send()
        sib_copy(n_chunk - 1).wait_send()
        for c in range(-n_low, 0):
            low_copy(c).wait_send()

    hop_send(last - 1, (last - 1) % 2).wait_send()
    back_send(last - 1, (last - 1) % 2).wait_send()
    back_send(last, last % 2).wait_send()

    @pl.when(s != last)
    def _():
        hop_send(last, last % 2).wait_send()

    pltpu.make_async_copy(hout.at[0], o_out.at[0], out_r).wait()

    @pl.when(s != 0)
    def _():
        pltpu.make_async_copy(gout.at[0], o_ig.at[0], ig_r).wait()

    for k in range(len(lines)):
        near, across, inner, outer = spots[k]

        @pl.when(inner)
        def _():
            def drain(c, carry):
                to_near, to_across = spot_copies(k, c)
                to_near.wait_send()
                to_across.wait_send()
                return carry

            lax.fori_loop(0, n_chunk, drain, 0)

    def drain_main(c, carry):
        here, there = finish_copies(c, w_place(c))
        here.wait()
        there.wait()
        return carry

    def drain_down(c, carry):
        here, there = finish_copies(c, d_place(c))
        here.wait()
        there.wait()
        return carry

    lax.fori_loop(0, n_main, drain_main, 0)
    lax.fori_loop(n_main, n_chunk, drain_down, 0)


def line_strides(n_dp):
    chips, stride, strides = n_dp // 2, 2, []
    while chips > 1:
        assert chips % 4 == 0
        strides.append(stride)
        stride, chips = stride * 4, chips // 4
    return strides


def on_device(n_sec, n_dp, patches, cot, positions, counts, gain, bias, wm, bm, sv, wd):
    _, tokens, width = patches.shape
    ff = wm.shape[2]
    lines = line_strides(n_dp)
    n_low = (ff // 2) // 256
    n_chunk = (width // 256) * (ff // width) + n_low
    tab = jnp.concatenate(
        [
            positions[0].astype(F32),
            jnp.broadcast_to(counts.astype(F32)[:, None], (1, tokens)),
            jnp.zeros((5, tokens), F32),
        ],
        axis=0,
    )[None]
    any_spec = pl.BlockSpec(memory_space=pl.ANY)
    vmem_spec = pl.BlockSpec(memory_space=pltpu.VMEM)
    image = (n_sec, tokens, width)
    wide = (n_sec, tokens, ff)
    dma = pltpu.SemaphoreType.DMA
    n_line = len(lines)
    scratch = [
        pltpu.VMEM(image, BF),
        pltpu.VMEM(image, BF),
        pltpu.VMEM(image, BF),
        pltpu.VMEM(wide, BF),
        pltpu.VMEM(wide, BF),
        pltpu.VMEM(wide, BF),
        pltpu.VMEM((width, ff), BF),
        pltpu.VMEM((ff, width), BF),
        pltpu.VMEM((n_sec, 2, tokens, width // 2), F32),
        pltpu.VMEM((n_sec, 8, tokens), F32),
        pltpu.VMEM((2, tokens, width), BF),
        pltpu.VMEM((2, tokens, width), BF),
        pltpu.VMEM((GROUP, GROUP), BF),
        pltpu.VMEM((8, 2 * width), F32),
        pltpu.VMEM((8, width // 2), F32),
        pltpu.VMEM((n_chunk, tokens // 2, width), BF),
        pltpu.VMEM((n_line, n_chunk, tokens // 2, width), BF),
        pltpu.VMEM((n_line, n_chunk, tokens // 2, width), BF),
        pltpu.VMEM((n_chunk + n_low, tokens // 2, width), BF),
        pltpu.VMEM((2, tokens, width), BF),
        pltpu.VMEM((8, width), F32),
        pltpu.VMEM((8, width), F32),
        pltpu.VMEM((n_line, 8, width), F32),
        pltpu.VMEM((n_line, 8, width), F32),
        dma((2,)),
        dma((n_sec,)),
        dma((n_sec,)),
        dma((n_sec,)),
        dma((n_sec,)),
        dma((n_sec,)),
        dma((n_sec + 2,)),
        dma((2,)),
        dma((2,)),
        dma,
        dma,
        dma((2,)),
        dma((n_chunk + n_low,)),
        dma((n_low,)),
        dma((n_low,)),
        dma((n_line, n_chunk)),
        dma((n_line, n_chunk)),
        dma((n_line, n_chunk)),
        dma((n_line, n_chunk)),
        dma((n_chunk,)),
        dma((n_chunk,)),
        dma((n_chunk,)),
        dma((1 + 2 * n_line,)),
        dma((1 + 2 * n_line,)),
    ]
    out, ig, gw, gd, small = pl.pallas_call(
        functools.partial(relay, n_sec, lines, tokens, width, ff),
        out_shape=(
            jax.ShapeDtypeStruct((1, tokens, width), BF),
            jax.ShapeDtypeStruct((1, tokens, width), BF),
            jax.ShapeDtypeStruct((width, ff), BF),
            jax.ShapeDtypeStruct((ff // 2, width), BF),
            jax.ShapeDtypeStruct((8, width), F32),
        ),
        in_specs=[any_spec, any_spec, vmem_spec, any_spec, any_spec] + [vmem_spec] * 4,
        out_specs=(any_spec, any_spec, any_spec, any_spec, vmem_spec),
        scratch_shapes=scratch,
        compiler_params=pltpu.CompilerParams(
            collective_id=0, has_side_effects=True, vmem_limit_bytes=63 * 2**20
        ),
    )(patches, cot, tab, wm, wd, gain, bias, bm, sv)
    return (
        out,
        ig,
        small[0:1],
        small[1:2],
        gw.astype(F32)[None],
        small[3:7].reshape(1, ff),
        small[2:3],
        gd.astype(F32)[None],
    )


def solution(mesh):
    n_sec, n_dp = mesh.shape["section"], mesh.shape["dp"]
    images = P(("section", "dp"), None, None)
    row = P("section", None)
    block = P("section", None, None)
    return jax.shard_map(
        functools.partial(on_device, n_sec, n_dp),
        mesh=mesh,
        in_specs=(images, images, images, P(("section", "dp")), row, row, block, row, row, block),
        out_specs=(images, images, row, row, block, row, row, block),
        check_vma=False,
    )
```

time: 1170 us -> 320 us (0.27)
  waiting for transfers between devices: 412 us -> 0 us
  Pallas kernels: 0 us -> 302 us
  other arithmetic: 213 us -> 11.4 us
  local copies, waits for them, and re-layouts: 156 us -> 4.45 us
  matrix products: 146 us -> 0 us
  blocking collectives: 97.3 us -> 0 us
  loops' own time: 60.2 us -> 0 us
  starting transfers between devices: 59.1 us -> 0 us
  between operations: 16 us -> 1.3 us
    pallas_call x0 -> x1, Pallas kernels: none -> 302 us  [on_device(): pl.pallas_call(functools.partial(relay, n_sec, lines, tokens, width, ff),...]
    ppermute x14 -> x0, waiting for transfers between devices: 196 us -> none  [shifted(): return lax.ppermute(x, axis, pairs)]
    psum x1 -> x0, waiting for transfers between devices: 186 us -> none  [on_device(): lax.psum(grad_matrix.astype(jnp.bfloat16), 'dp').astype(jnp.float32)]
    dot_general x56 -> x0, matrix products: 128 us -> none  [the longest x8 36.6 us: mixer_core(): jnp.dot(normed_low, matrix[:, :3 * model_width], preferred_element_type=j...]
    all_gather x1 -> x0, blocking collectives: 69.9 us -> none  [on_device(): lax.all_gather(table_local, 'section', axis=0, tiled=True)]
    another operation x14 -> x0, loops' own time: 60.2 us -> none  [the longest x7 32 us: on_device(): lax.switch(branch_index, forward_fns, section_in.astype(jnp.float32), tok...]
    concatenate x17 -> x0, other arithmetic: 59.2 us -> none  [the longest x4 35 us: mixer_backward(): jnp.concatenate([grad_in_w, grad_out_w], axis=1)]
    another operation x25 -> x0, local copies, waits for them, and re-layouts: 53.7 us -> none
  transfers between devices with their start and end apart: 19 -> 0, of which waited for: 14 -> 0; matrix products, arithmetic and copies ran while one was open for 6% -> 0% of each run, Pallas kernels for 0% -> 0%
where the time goes in v1:
time: 320 us
  Pallas kernels  302 us (94%)
  other arithmetic  11.4 us (4%)
  local copies, waits for them, and re-layouts  4.45 us (1%)
    pallas_call x1, Pallas kernels, on_device(): pl.pallas_call(functools.partial(relay, n_sec, lines, tokens, width, ff),...  302 us
    broadcast_in_dim x1, other arithmetic, on_device(): gw.astype(F32)[None]  7.52 us

profile of v1, /device:TPU:0, one launch (start us, length us, event | category | flops | bytes accessed | tf_op | source)
XLA Modules:
  0.0 319.6 jit_solution(11593381936063820960)
XLA Ops:
  0.6 0.7 convert_bitcast_fusion
  2.0 0.1 pad.1.clone
  2.0 0.1 pad.2.clone
  2.1 0.7 maximum_bitcast_fusion.tab
  2.8 302.5 %shard_map.161 = (bf16[1,256,768]{2,1,0:T(8,128)(2,1)}, bf16[1,256,768]{2,1,0:T(8,128)(2,1)}, bf16[768,3072]{1,0:T(8,128)(2,1)}, bf16[1536,768]{1,0:T(8,128)(2,1)}, f32[8,768]{1,0:T(8,128)}) custom-call(bf16[1,256,768]{2,1,0:T(8,128)(2,1)} %patches.1, bf16[1,256,768]{2,1,0:T(8,128)(2,1)} %cot.1, f32[1,8,256]{2,1,0:T(8,128)} %maximum_bitcast_fusion.tab, ...), custom_call_target="tpu_custom_call" | custom-call | tf_op jit(solution)/shard_map/pallas_call | solution.py:775
  305.3 1.4 fusion
  306.7 0.7 slice_bitcast_fusion
  307.5 0.6 copy.18
  308.1 0.0 copy-start
  308.1 7.5 %bitcast_convert_fusion = f32[1,768,3072]{2,1,0:T(8,128)} fusion(bf16[768,3072]{1,0:T(8,128)(2,1)} %get-tuple-element.16), kind=kLoop, calls=%fused_computation | loop fusion | flops 2359296 | bytes 14155776 | tf_op jit(solution)/shard_map/broadcast_in_dim | solution.py:796
  315.6 0.0 copy-start.2
  315.6 0.0 copy-start.1
  315.6 0.0 copy-done
  315.6 2.5 bitcast_convert_fusion.1
  318.1 0.0 copy-done.2
  318.1 0.7 copy.22
  318.9 0.0 copy-done.1
  318.9 0.7 copy.23
  (1 shorter events, 0.0 us)
Async XLA Ops:
  308.1 7.5 %copy-start = (bf16[1536,768]{1,0:T(8,128)(2,1)S(1)}, bf16[1536,768]{1,0:T(8,128)(2,1)}, u32[]{:S(2)}) copy-start(bf16[1536,768]{1,0:T(8,128)(2,1)} %get-tuple-element.17) | copy-start | bytes 7077892
  315.6 2.6 copy-start.2
  315.6 3.3 %copy-start.1 = (bf16[1,256,768]{2,1,0:T(8,128)(2,1)S(1)}, bf16[1,256,768]{2,1,0:T(8,128)(2,1)}, u32[]{:S(2)}) copy-start(bf16[1,256,768]{2,1,0:T(8,128)(2,1)} %get-tuple-element.30) | copy-start | bytes 1179652

commit v2 on v1

--- a/solution.py
+++ b/solution.py
@@ -15,7 +15,8 @@
 BF = jnp.bfloat16
 F32 = jnp.float32
 HI = lax.Precision.HIGHEST
-LAG_SIB, LAG_ONE, LAG_TWO, LAG_END = 1, 2, 4, 6
+LAG_SIB, LAG_ONE, LAG_TWO, LAG_END = 1, 3, 6, 9
+N_SUB = 2
 
 
 def nn(a, b, precision=None):
@@ -42,7 +43,7 @@
     o_out, o_ig, o_w, o_d, o_small,
     hin, gin, act, big1, big2, big3, wv, dv, cs, tabs, hout, gout, perm, bqk, freq,
     mine, zin, pin, sib, tmp, sg, sg_sib, sg_one, sg_two,
-    w_sem, hin_r, gin_r, tab_r, hop_s, gop_s, ini_s, wd_s, wd_r, out_r, ig_r,
+    w_sem, hin_r, gin_r, tab_r, hop_s, gop_s, ini_s, cot_r, wd_s, wd_r, out_r, ig_r,
     sib_s, sib_r, low_s, mine_r, za_s, zin_r, pb_s, pin_r, fin_l, fin_s, fin_r, sg_s, sg_r,
 ):
     s = lax.axis_index("section")
@@ -56,6 +57,7 @@
     n_main = (width // 256) * (ff // width)
     n_low = (ff // 2) // 256
     n_chunk = n_main + n_low
+    n_sub = N_SUB
     score_scale = HEAD_DIM ** (-0.5)
 
     def to_section(target):
@@ -115,31 +117,83 @@
     patch_own = pltpu.make_async_copy(patches.at[0], hin.at[0], hin_r.at[0])
     cot_send = remote(cot.at[0], gin.at[s], ini_s.at[n_sec + 1], gin_r.at[s], to_section(last))
     cot_own = pltpu.make_async_copy(cot.at[0], gin.at[last], gin_r.at[last])
+    cot_out = remote(cot.at[0], gout.at[0], ini_s.at[n_sec + 1], cot_r, to_section(last - 1))
+    cot_on = remote(gout.at[0], gin.at[0], ini_s.at[n_sec + 2], gin_r.at[0], to_section(last))
 
     @pl.when(s == 0)
     def _():
         patch_own.start()
+        cot_out.start()
 
     @pl.when(s != 0)
     def _():
         patch_send.start()
 
+    @pl.when((s != 0) & (s != last))
+    def _():
+        cot_send.start()
+
     @pl.when(s == last)
     def _():
         cot_own.start()
 
-    down_half = (ff // 2) // 2
-    mine_rows = pl.ds(pl.multiple_of(core * down_half, down_half), down_half)
-    their_rows = pl.ds(pl.multiple_of((1 - core) * down_half, down_half), down_half)
-    down_send = remote(
-        wd.at[0, mine_rows], dv.at[mine_rows], wd_s.at[0], wd_r.at[0], to_section(lax.rem(s + 1, n_sec))
-    )
-    down_pass = remote(dv.at[mine_rows], dv.at[mine_rows], wd_s.at[1], wd_r.at[1], to_dp(other))
-    down_pass_in = remote(dv.at[their_rows], dv.at[their_rows], wd_s.at[1], wd_r.at[1], to_dp(other))
+    near0 = spots[0][0]
+    side = lax.rem(d // lines[0], 2)
+    n_part = 4
+    part = (ff // 2) // 4 // n_part
+
+    def down_rows(which_side, which_core, k):
+        start = (which_side * 2 + which_core) * (n_part * part) + k * part
+        return pl.ds(pl.multiple_of(start, part), part)
+
+    def down_send(k):
+        rows = down_rows(side, core, k)
+        return remote(wd.at[0, rows], dv.at[rows], wd_s.at[0, k], wd_r.at[0, k], to_section(lax.rem(s + 1, n_sec)))
+
+    def down_near(k):
+        rows = down_rows(side, core, k)
+        return remote(dv.at[rows], dv.at[rows], wd_s.at[1, k], wd_r.at[1, k], to_dp(near0))
+
+    def down_pass(k):
+        rows = down_rows(side, core, k)
+        return remote(dv.at[rows], dv.at[rows], wd_s.at[2, k], wd_r.at[2, k], to_dp(other))
+
+    def down_pass_far(k):
+        rows = down_rows(1 - side, core, k)
+        return remote(dv.at[rows], dv.at[rows], wd_s.at[3, k], wd_r.at[3, k], to_dp(other))
 
     @pl.when(even)
     def _():
-        down_send.start()
+        for k in range(n_part):
+            down_send(k).start()
+
+    def table(i):
+        pltpu.make_async_copy(tab.at[0], tabs.at[i], tab_r.at[i]).wait()
+        angle = nn(jnp.transpose(tabs[i]), freq[...], HI)
+        cs[i, 0] = jnp.cos(angle)
+        cs[i, 1] = jnp.sin(angle)
+
+    ahead = (s == 0) & (core == 0)
+
+    @pl.when(even)
+    def _():
+        freq[...] = jnp.zeros_like(freq)
+        freq[0:1, :] = sv[:, : width // 2]
+        freq[1:2, :] = sv[:, width // 2 :]
+
+        def early(i, carry):
+            @pl.when((i == 0) | jnp.logical_not(ahead))
+            def _():
+                table(i)
+
+            return carry
+
+        lax.fori_loop(0, n_sec, early, 0)
+
+    @pl.when(odd)
+    def _():
+        for i in range(n_sec):
+            pltpu.make_async_copy(tab.at[0], tabs.at[i], tab_r.at[i]).wait()
 
     sg[...] = jnp.zeros_like(sg)
     load_w.wait()
@@ -156,9 +210,18 @@
             wv[:, columns] = nn(wv[:, columns], table).astype(BF)
             row = jnp.broadcast_to(bm[:, columns], (8, GROUP))
             bqk[:, columns] = nn(row, table.astype(F32), HI)
-        freq[...] = jnp.zeros_like(freq)
-        freq[0:1, :] = sv[:, : width // 2]
-        freq[1:2, :] = sv[:, width // 2 :]
+
+    @pl.when(s == last - 1)
+    def _():
+        cot_out.wait_recv()
+        cot_on.start()
+
+    @pl.when(odd)
+    def _():
+        for k in range(n_part):
+            down_send(k).wait_recv()
+            down_near(k).start()
+            down_pass(k).start()
 
     lane = lax.broadcasted_iota(jnp.int32, (1, GROUP), 1)
     q_masks = [((lane & 127) >> 5) == e for e in range(4)]
@@ -184,9 +247,6 @@
         xhat, _ = normalise(x)
         a = (xhat * gain[...] + bias[...]).astype(BF)
         act[i] = a
-        angle = nn(jnp.transpose(tabs[i]), freq[...], HI)
-        cs[i, 0] = jnp.cos(angle)
-        cs[i, 1] = jnp.sin(angle)
         keys_on = key_mask(i)
         for g in range(n_group):
             cosine = cs[i, 0, :, g * pairs : (g + 1) * pairs]
@@ -293,9 +353,12 @@
         @pl.when(i == 0)
         def _():
             load_d.wait()
-            down_send.wait_recv()
-            down_pass.start()
-            down_pass_in.wait_recv()
+            for k in range(n_part):
+                down_near(k).wait_recv()
+                down_pass_far(k).start()
+            for k in range(n_part):
+                down_pass(k).wait_recv()
+                down_pass_far(k).wait_recv()
 
         branch = nn(big1[i], dv[...]) + sv[...]
         hout[slot] = (x + row_mask(i) * branch).astype(BF)
@@ -330,42 +393,30 @@
         return remote(gout.at[slot], o_ig.at[0], gop_s.at[i], ig_r, to_section(i))
 
     def forward(i):
-        slot = lax.rem(i, 2)
-
-        @pl.when(i >= 2)
-        def _():
-            hop_send(i - 2, slot).wait_send()
-
-        hop_send(i, slot).wait_recv()
-        tab_own_like = pltpu.make_async_copy(tab.at[0], tabs.at[i], tab_r.at[i])
-        tab_own_like.wait()
+        hop_send(i, i).wait_recv()
 
         @pl.when(even)
         def _():
-            attention_forward(i, slot)
+            attention_forward(i, i)
 
         @pl.when(odd)
         def _():
-            dense_forward(i, slot)
+            dense_forward(i, i)
+
+        @pl.when((s != last) & (i >= 1))
+        def _():
+            hop_send(i - 1, i - 1).wait_send()
 
         @pl.when(s != last)
         def _():
-            hop_send(i, slot).start()
-
-        @pl.when((s == last) & (i != last))
-        def _():
-            result_send(i, slot).start()
-
-        @pl.when((s == last) & (i == last))
-        def _():
-            pltpu.make_async_copy(hout.at[slot], o_out.at[0], out_r).start()
+            hop_send(i, i).start()
 
     def backward(i):
         slot = lax.rem(i, 2)
 
-        @pl.when((i == 3) | ((i == 2) & (s != 0)))
-        def _():
-            back_send(i - 2, slot).wait_send()
+        @pl.when((i == 0) & (s == last - 1))
+        def _():
+            cot_on.wait_send()
 
         @pl.when((i == 2) & (s == 0))
         def _():
@@ -381,6 +432,10 @@
         def _():
             dense_backward(i, slot)
 
+        @pl.when((i >= 2) | ((i == 1) & (s != 0)))
+        def _():
+            back_send(i - 1, 1 - slot).wait_send()
+
         @pl.when(s != 0)
         def _():
             back_send(i, slot).start()
@@ -394,23 +449,30 @@
             pltpu.make_async_copy(gout.at[slot], o_ig.at[0], ig_r).start()
 
     def tick(j, carry):
-        @pl.when(j < n_sec)
-        def _():
-            forward(j)
-
-        @pl.when((s != last) & (((s == 0) & (j == 2)) | ((s != 0) & (j == 0))))
-        def _():
-            cot_send.start()
-
-        b = j - (last - s)
-
-        @pl.when((b >= 0) & (b < n_sec))
-        def _():
-            backward(b)
+        is_forward = jnp.where(s == last, lax.rem(j, 2) == 0, j < n_sec)
+        i = jnp.where(s == last, j // 2, lax.rem(j, n_sec))
+
+        @pl.when(is_forward)
+        def _():
+            forward(i)
+
+        @pl.when(ahead & (j == 0))
+        def _():
+            lax.fori_loop(1, n_sec, lambda i, carry: (table(i), carry)[1], 0)
+
+        @pl.when(jnp.logical_not(is_forward))
+        def _():
+            backward(i)
 
         return carry
 
-    lax.fori_loop(0, 2 * n_sec - 1, tick, 0)
+    lax.fori_loop(0, 2 * n_sec, tick, 0)
+
+    @pl.when(s == last)
+    def _():
+        for i in range(last):
+            result_send(i, i).start()
+        pltpu.make_async_copy(hout.at[last], o_out.at[0], out_r).start()
 
     @pl.when(even)
     def _():
@@ -421,13 +483,9 @@
             part = jnp.broadcast_to(sg[row : row + 1, lo : lo + GROUP], (8, GROUP))
             sg[row : row + 1, lo : lo + GROUP] = nt(part, back, HI)[0:1]
 
-    my_half = pl.ds(pl.multiple_of(core * half, half), half)
-    their_half = pl.ds(pl.multiple_of((1 - core) * half, half), half)
+    my_half = pl.ds(core * n_sub, n_sub)
+    their_half = pl.ds((1 - core) * n_sub, n_sub)
     shift = jnp.where(odd, n_low, 0)
-    steps = n_chunk + n_low + len(lines) * LAG_END + 1
-
-    def flat(ref):
-        return ref.reshape(n_sec * tokens, ref.shape[-1])
 
     def sib_slot(c):
         return jnp.where(c < 0, n_chunk + n_low + c, c)
@@ -440,7 +498,11 @@
     def low_copy(c):
         at = c + n_low
         return remote(
-            sib.at[n_chunk + at], mine.at[n_main + at], low_s.at[at], mine_r.at[at], to_section(lax.rem(s + last, n_sec))
+            sib.at[n_chunk + at],
+            mine.at[pl.ds((n_main + at) * n_sub, n_sub)],
+            low_s.at[at],
+            mine_r.at[at],
+            to_section(lax.rem(s + last, n_sec)),
         )
 
     def make_block(c):
@@ -455,20 +517,26 @@
         is_main = (c >= 0) & (c < n_main)
         from_act = is_main & (odd | (column < 3))
 
+        def keep(block):
+            tmp[slot] = block.astype(BF).reshape(2 * n_sub, half // n_sub, width)
+
         @pl.when(from_act)
         def _():
             rows = pl.ds(pl.multiple_of(row * 256, 256), 256)
             columns = pl.ds(pl.multiple_of(column * width, width), width)
             left = act[:, :, rows].reshape(n_sec * tokens, 256)
             right = big3[:, :, columns].reshape(n_sec * tokens, width)
-            tmp[slot] = tn(left, right).astype(BF)
+            keep(tn(left, right))
 
         @pl.when(from_act & even & (column < 2))
         def _():
             back = perm[...]
-            for block in range(width // GROUP):
-                at = slice(block * GROUP, (block + 1) * GROUP)
-                tmp[slot, :, at] = nt(tmp[slot, :, at], back).astype(BF)
+            held = tmp[slot].reshape(2 * half, width)
+            keep(
+                jnp.concatenate(
+                    [nt(held[:, k * GROUP : (k + 1) * GROUP], back) for k in range(width // GROUP)], axis=1
+                )
+            )
 
         @pl.when(jnp.logical_not(from_act))
         def _():
@@ -477,123 +545,51 @@
             rows = pl.ds(pl.multiple_of(start, 256), 256)
             left = big1[:, :, rows].reshape(n_sec * tokens, 256)
             right = gin[...].reshape(n_sec * tokens, width)
-            tmp[slot] = tn(left, right).astype(BF)
+            keep(tn(left, right))
 
         sib_copy(c).start()
 
-    def spot_copies(k, c):
+    def spot_copies(k, u):
         near, across, inner, outer = spots[k]
-        to_near = remote(mine.at[c], zin.at[k, c], za_s.at[k, c], zin_r.at[k, c], to_dp(near))
-        to_across = remote(zin.at[k, c], pin.at[k, c], pb_s.at[k, c], pin_r.at[k, c], to_dp(across))
+        to_near = remote(mine.at[u], zin.at[k, u], za_s.at[k, u], zin_r.at[k, u], to_dp(near))
+        to_across = remote(zin.at[k, u], pin.at[k, u], pb_s.at[k, u], pin_r.at[k, u], to_dp(across))
         return to_near, to_across
 
-    def result_place(c):
-        return c
-
-    def w_place(c):
+    piece_rows = half // n_sub
+
+    def w_place(u):
+        c = u // n_sub
         row = c // (ff // width)
         column = lax.rem(c, ff // width)
-        rows = pl.ds(pl.multiple_of(row * 256 + core * half, half), half)
+        start = row * 256 + core * half + lax.rem(u, n_sub) * piece_rows
+        rows = pl.ds(pl.multiple_of(start, piece_rows), piece_rows)
         columns = pl.ds(pl.multiple_of(column * width, width), width)
         return o_w.at[rows, columns]
 
-    def d_place(c):
-        rows = pl.ds(pl.multiple_of((c - n_main) * 256 + core * half, half), half)
-        return o_d.at[rows, :]
-
-    def finish_copies(c, place):
-        here = pltpu.make_async_copy(mine.at[c], place, fin_l.at[c])
-        there = remote(mine.at[c], place, fin_s.at[c], fin_r.at[c], to_dp(other))
+    def d_place(u):
+        c = u // n_sub
+        start = (c - n_main) * 256 + core * half + lax.rem(u, n_sub) * piece_rows
+        return o_d.at[pl.ds(pl.multiple_of(start, piece_rows), piece_rows), :]
+
+    def finish_copies(u, place):
+        here = pltpu.make_async_copy(mine.at[u], place, fin_l.at[u])
+        there = remote(mine.at[u], place, fin_s.at[u], fin_r.at[u], to_dp(other))
         return here, there
 
-    def finish(c):
-        @pl.when(c < n_main)
-        def _():
-            here, there = finish_copies(c, w_place(c))
+    def finish(u):
+        @pl.when(u < n_main * n_sub)
+        def _():
+            here, there = finish_copies(u, w_place(u))
             here.start()
             there.start()
 
-        @pl.when(c >= n_main)
-        def _():
-            here, there = finish_copies(c, d_place(c))
+        @pl.when(u >= n_main * n_sub)
+        def _():
+            here, there = finish_copies(u, d_place(u))
             here.start()
             there.start()
 
-    def sum_step(t, carry):
-        c = t - shift
-
-        @pl.when((even & (c < n_main)) | (odd & (c < n_chunk)))
-        def _():
-            make_block(c)
-
-        c1 = c - LAG_SIB
-
-        @pl.when((even & (c1 >= 0) & (c1 < n_main)) | (odd & (c1 >= -n_low) & (c1 < n_chunk)))
-        def _():
-            slot = lax.rem(c1 + n_low, 2)
-            at = sib_slot(c1)
-            sib_copy(c1).wait_recv()
-            total = (tmp[slot, my_half].astype(F32) + sib[at].astype(F32)).astype(BF)
-
-            @pl.when(c1 < 0)
-            def _():
-                sib[at] = total
-                low_copy(c1).start()
-
-            @pl.when(c1 >= 0)
-            def _():
-                mine[c1] = total
-
-        @pl.when(even & (c1 >= n_main) & (c1 < n_chunk))
-        def _():
-            low_copy(c1 - n_chunk).wait_recv()
-
-        for k in range(len(lines)):
-            near, across, inner, outer = spots[k]
-            base = LAG_SIB + k * LAG_END
-            c0 = c - base
-
-            @pl.when(outer & (c0 >= 0) & (c0 < n_chunk))
-            def _():
-                to_near, _ = spot_copies(k, c0)
-                to_near.start()
-
-            c2 = c - base - LAG_ONE
-
-            @pl.when(inner & (c2 >= 0) & (c2 < n_chunk))
-            def _():
-                to_near, to_across = spot_copies(k, c2)
-                to_near.wait_recv()
-                zin[k, c2] = (mine[c2].astype(F32) + zin[k, c2].astype(F32)).astype(BF)
-                to_across.start()
-
-            c3 = c - base - LAG_TWO
-
-            @pl.when(inner & (c3 >= 0) & (c3 < n_chunk))
-            def _():
-                to_near, to_across = spot_copies(k, c3)
-                to_across.wait_recv()
-                mine[c3] = (zin[k, c3].astype(F32) + pin[k, c3].astype(F32)).astype(BF)
-                to_near.start()
-                if k == len(lines) - 1:
-                    finish(c3)
-
-            c4 = c - base - LAG_END
-
-            @pl.when(outer & (c4 >= 0) & (c4 < n_chunk))
-            def _():
-                to_near, _ = spot_copies(k, c4)
-                to_near.wait()
-                mine[c4] = zin[k, c4]
-                if k == len(lines) - 1:
-                    finish(c4)
-
-        return carry
-
     small_sib = remote(sg, sg_sib, sg_s.at[0], sg_r.at[0], to_dp(other))
-    small_sib.start()
-    small_sib.wait()
-    sg[...] = sg[...] + sg_sib[...]
 
     def small_copies(k):
         near, across, inner, outer = spots[k]
@@ -601,29 +597,120 @@
         to_across = remote(sg_one.at[k], sg_two.at[k], sg_s.at[2 + 2 * k], sg_r.at[2 + 2 * k], to_dp(across))
         return to_near, to_across
 
-    for k in range(len(lines)):
-        near, across, inner, outer = spots[k]
-        to_near, to_across = small_copies(k)
-
-        @pl.when(outer)
-        def _():
-            to_near.start()
-            to_near.wait()
-            sg[...] = sg_one[k]
-
-        @pl.when(inner)
-        def _():
-            to_near.wait_recv()
-            sg_one[k] = sg[...] + sg_one[k]
-            to_across.start()
-            to_across.wait()
-            sg[...] = sg_one[k] + sg_two[k]
-            to_near.start()
-            to_near.wait_send()
-
+    n_unit = n_chunk * n_sub
+    steps = n_unit + n_low * n_sub + n_sub * LAG_SIB + len(lines) * LAG_END + 1
+
+    def sum_step(t, carry):
+        v = t - shift * n_sub
+        c = v // n_sub
+
+        @pl.when((lax.rem(t, n_sub) == 0) & ((even & (c < n_main)) | (odd & (c < n_chunk))))
+        def _():
+            make_block(t // n_sub - shift)
+
+        c1 = t // n_sub - shift - LAG_SIB
+        first = lax.rem(t, n_sub) == 0
+
+        @pl.when(first & ((even & (c1 >= 0) & (c1 < n_main)) | (odd & (c1 >= -n_low) & (c1 < n_chunk))))
+        def _():
+            slot = lax.rem(c1 + n_low, 2)
+            at = sib_slot(c1)
+            sib_copy(c1).wait_recv()
+            total = (tmp[slot, my_half].astype(F32) + sib[at].astype(F32)).astype(BF)
+
+            @pl.when(c1 < 0)
+            def _():
+                sib[at] = total
+                low_copy(c1).start()
+
+            @pl.when(c1 >= 0)
+            def _():
+                mine[pl.ds(c1 * n_sub, n_sub)] = total
+
+        @pl.when(first & even & (c1 >= n_main) & (c1 < n_chunk))
+        def _():
+            low_copy(c1 - n_chunk).wait_recv()
+
+        @pl.when(t == 0)
+        def _():
+            small_sib.start()
+
+        @pl.when(t == 2)
+        def _():
+            small_sib.wait()
+            sg[...] = sg[...] + sg_sib[...]
+
+        for k in range(len(lines)):
+            near, across, inner, outer = spots[k]
+            small_near, small_across = small_copies(k)
+            at = 2 + 9 * k
+
+            @pl.when(outer & (t == at))
+            def _():
+                small_near.start()
+
+            @pl.when(inner & (t == at + 3))
+            def _():
+                small_near.wait_recv()
+                sg_one[k] = sg[...] + sg_one[k]
+                small_across.start()
+
+            @pl.when(inner & (t == at + 6))
+            def _():
+                small_across.wait()
+                sg[...] = sg_one[k] + sg_two[k]
+                small_near.start()
+                small_near.wait_send()
+
+            @pl.when(outer & (t == at + 9))
+            def _():
+                small_near.wait()
+                sg[...] = sg_one[k]
+
+        for k in range(len(lines)):
+            near, across, inner, outer = spots[k]
+            base = LAG_SIB * n_sub + k * LAG_END
+            u0 = v - base
+
+            @pl.when(outer & (u0 >= 0) & (u0 < n_unit))
+            def _():
+                to_near, _ = spot_copies(k, u0)
+                to_near.start()
+
+            u2 = v - base - LAG_ONE
+
+            @pl.when(inner & (u2 >= 0) & (u2 < n_unit))
+            def _():
+                to_near, to_across = spot_copies(k, u2)
+                to_near.wait_recv()
+                zin[k, u2] = (mine[u2].astype(F32) + zin[k, u2].astype(F32)).astype(BF)
+                to_across.start()
+
+            u3 = v - base - LAG_TWO
+
+            @pl.when(inner & (u3 >= 0) & (u3 < n_unit))
+            def _():
+                to_near, to_across = spot_copies(k, u3)
+                to_across.wait_recv()
+                mine[u3] = (zin[k, u3].astype(F32) + pin[k, u3].astype(F32)).astype(BF)
+                to_near.start()
+                if k == len(lines) - 1:
+                    finish(u3)
+
+            u4 = v - base - LAG_END
+
+            @pl.when(outer & (u4 >= 0) & (u4 < n_unit))
+            def _():
+                to_near, _ = spot_copies(k, u4)
+                to_near.wait()
+                mine[u4] = zin[k, u4]
+                if k == len(lines) - 1:
+                    finish(u4)
+
+        return carry
+
+    lax.fori_loop(0, steps, sum_step, 0)
     o_small[...] = sg[...]
-
-    lax.fori_loop(0, steps, sum_step, 0)
 
     for send in tab_sends:
         send.wait_send()
@@ -638,25 +725,32 @@
 
     @pl.when(even)
     def _():
-        down_send.wait_send()
+        for k in range(n_part):
+            down_send(k).wait_send()
         sib_copy(n_main - 2).wait_send()
         sib_copy(n_main - 1).wait_send()
 
     @pl.when(odd)
     def _():
-        down_pass.wait_send()
+        for k in range(n_part):
+            down_near(k).wait_send()
+            down_pass(k).wait_send()
+            down_pass_far(k).wait_send()
         sib_copy(n_chunk - 2).wait_send()
         sib_copy(n_chunk - 1).wait_send()
         for c in range(-n_low, 0):
             low_copy(c).wait_send()
 
-    hop_send(last - 1, (last - 1) % 2).wait_send()
-    back_send(last - 1, (last - 1) % 2).wait_send()
     back_send(last, last % 2).wait_send()
 
     @pl.when(s != last)
     def _():
-        hop_send(last, last % 2).wait_send()
+        hop_send(last, last).wait_send()
+
+    @pl.when(s == last)
+    def _():
+        for i in range(last):
+            result_send(i, i).wait_send()
 
     pltpu.make_async_copy(hout.at[0], o_out.at[0], out_r).wait()
 
@@ -669,28 +763,28 @@
 
         @pl.when(inner)
         def _():
-            def drain(c, carry):
-                to_near, to_across = spot_copies(k, c)
+            def drain(u, carry):
+                to_near, to_across = spot_copies(k, u)
                 to_near.wait_send()
                 to_across.wait_send()
                 return carry
 
-            lax.fori_loop(0, n_chunk, drain, 0)
-
-    def drain_main(c, carry):
-        here, there = finish_copies(c, w_place(c))
+            lax.fori_loop(0, n_unit, drain, 0)
+
+    def drain_main(u, carry):
+        here, there = finish_copies(u, w_place(u))
         here.wait()
         there.wait()
         return carry
 
-    def drain_down(c, carry):
-        here, there = finish_copies(c, d_place(c))
+    def drain_down(u, carry):
+        here, there = finish_copies(u, d_place(u))
         here.wait()
         there.wait()
         return carry
 
-    lax.fori_loop(0, n_main, drain_main, 0)
-    lax.fori_loop(n_main, n_chunk, drain_down, 0)
+    lax.fori_loop(0, n_main * n_sub, drain_main, 0)
+    lax.fori_loop(n_main * n_sub, n_unit, drain_down, 0)
 
 
 def line_strides(n_dp):
@@ -708,6 +802,7 @@
     lines = line_strides(n_dp)
     n_low = (ff // 2) // 256
     n_chunk = (width // 256) * (ff // width) + n_low
+    n_unit, rows = n_chunk * N_SUB, 128 // N_SUB
     tab = jnp.concatenate(
         [
             positions[0].astype(F32),
@@ -733,16 +828,16 @@
         pltpu.VMEM((ff, width), BF),
         pltpu.VMEM((n_sec, 2, tokens, width // 2), F32),
         pltpu.VMEM((n_sec, 8, tokens), F32),
-        pltpu.VMEM((2, tokens, width), BF),
+        pltpu.VMEM(image, BF),
         pltpu.VMEM((2, tokens, width), BF),
         pltpu.VMEM((GROUP, GROUP), BF),
         pltpu.VMEM((8, 2 * width), F32),
         pltpu.VMEM((8, width // 2), F32),
-        pltpu.VMEM((n_chunk, tokens // 2, width), BF),
-        pltpu.VMEM((n_line, n_chunk, tokens // 2, width), BF),
-        pltpu.VMEM((n_line, n_chunk, tokens // 2, width), BF),
-        pltpu.VMEM((n_chunk + n_low, tokens // 2, width), BF),
-        pltpu.VMEM((2, tokens, width), BF),
+        pltpu.VMEM((n_unit, rows, width), BF),
+        pltpu.VMEM((n_line, n_unit, rows, width), BF),
+        pltpu.VMEM((n_line, n_unit, rows, width), BF),
+        pltpu.VMEM((n_chunk + n_low, N_SUB, rows, width), BF),
+        pltpu.VMEM((2, 2 * N_SUB, rows, width), BF),
         pltpu.VMEM((8, width), F32),
         pltpu.VMEM((8, width), F32),
         pltpu.VMEM((n_line, 8, width), F32),
@@ -753,22 +848,23 @@
         dma((n_sec,)),
         dma((n_sec,)),
         dma((n_sec,)),
-        dma((n_sec + 2,)),
-        dma((2,)),
-        dma((2,)),
+        dma((n_sec + 3,)),
+        dma,
+        dma((4, 4)),
+        dma((4, 4)),
         dma,
         dma,
         dma((2,)),
         dma((n_chunk + n_low,)),
         dma((n_low,)),
         dma((n_low,)),
-        dma((n_line, n_chunk)),
-        dma((n_line, n_chunk)),
-        dma((n_line, n_chunk)),
-        dma((n_line, n_chunk)),
-        dma((n_chunk,)),
-        dma((n_chunk,)),
-        dma((n_chunk,)),
+        dma((n_line, n_unit)),
+        dma((n_line, n_unit)),
+        dma((n_line, n_unit)),
+        dma((n_line, n_unit)),
+        dma((n_unit,)),
+        dma((n_unit,)),
+        dma((n_unit,)),
         dma((1 + 2 * n_line,)),
         dma((1 + 2 * n_line,)),
     ]

time: 320 us -> 260 us (0.81)
  Pallas kernels: 302 us -> 243 us
    pallas_call x1, Pallas kernels: 302 us -> 243 us  [on_device(): pl.pallas_call(functools.partial(relay, n_sec, lines, tokens, width, ff),...]
where the time goes in v2:
time: 260 us
  Pallas kernels  243 us (93%)
  other arithmetic  11.4 us (4%)
  local copies, waits for them, and re-layouts  4.45 us (2%)
    pallas_call x1, Pallas kernels, on_device(): pl.pallas_call(functools.partial(relay, n_sec, lines, tokens, width, ff),...  243 us
    broadcast_in_dim x1, other arithmetic, on_device(): gw.astype(F32)[None]  7.52 us

profile of v2, /device:TPU:0, one launch (start us, length us, event | category | flops | bytes accessed | tf_op | source)
XLA Modules:
  0.0 259.8 jit_solution(1656414962539796967)
XLA Ops:
  0.6 0.7 convert_bitcast_fusion
  2.0 0.1 pad.1.clone
  2.0 0.1 pad.2.clone
  2.1 0.7 maximum_bitcast_fusion.tab
  2.8 242.6 %shard_map.161 = (bf16[1,256,768]{2,1,0:T(8,128)(2,1)}, bf16[1,256,768]{2,1,0:T(8,128)(2,1)}, bf16[768,3072]{1,0:T(8,128)(2,1)}, bf16[1536,768]{1,0:T(8,128)(2,1)}, f32[8,768]{1,0:T(8,128)}) custom-call(bf16[1,256,768]{2,1,0:T(8,128)(2,1)} %patches.1, bf16[1,256,768]{2,1,0:T(8,128)(2,1)} %cot.1, f32[1,8,256]{2,1,0:T(8,128)} %maximum_bitcast_fusion.tab, ...), custom_call_target="tpu_custom_call" | custom-call | tf_op jit(solution)/shard_map/pallas_call | solution.py:871
  245.4 1.4 fusion
  246.9 0.7 slice_bitcast_fusion
  247.6 0.6 copy.18
  248.2 0.0 copy-start
  248.2 7.5 %bitcast_convert_fusion = f32[1,768,3072]{2,1,0:T(8,128)} fusion(bf16[768,3072]{1,0:T(8,128)(2,1)} %get-tuple-element.16), kind=kLoop, calls=%fused_computation | loop fusion | flops 2359296 | bytes 14155776 | tf_op jit(solution)/shard_map/broadcast_in_dim | solution.py:892
  255.7 0.0 copy-start.2
  255.8 0.0 copy-start.1
  255.8 0.0 copy-done
  255.8 2.5 bitcast_convert_fusion.1
  258.3 0.0 copy-done.2
  258.3 0.7 copy.22
  259.1 0.0 copy-done.1
  259.1 0.7 copy.23
  (1 shorter events, 0.0 us)
Async XLA Ops:
  248.2 7.5 %copy-start = (bf16[1536,768]{1,0:T(8,128)(2,1)S(1)}, bf16[1536,768]{1,0:T(8,128)(2,1)}, u32[]{:S(2)}) copy-start(bf16[1536,768]{1,0:T(8,128)(2,1)} %get-tuple-element.17) | copy-start | bytes 7077892
  255.7 2.6 copy-start.2
  255.8 3.3 %copy-start.1 = (bf16[1,256,768]{2,1,0:T(8,128)(2,1)S(1)}, bf16[1,256,768]{2,1,0:T(8,128)(2,1)}, u32[]{:S(2)}) copy-start(bf16[1,256,768]{2,1,0:T(8,128)(2,1)} %get-tuple-element.30) | copy-start | bytes 1179652

commit v3 on v2

--- a/solution.py
+++ b/solution.py
@@ -15,8 +15,10 @@
 BF = jnp.bfloat16
 F32 = jnp.float32
 HI = lax.Precision.HIGHEST
-LAG_SIB, LAG_ONE, LAG_TWO, LAG_END = 1, 3, 6, 9
+LAG_SIB, LAG_ONE, LAG_TWO, LAG_END = 1, 2, 4, 6
 N_SUB = 2
+SLOTS = 8
+N_AWAY = 3
 
 
 def nn(a, b, precision=None):
@@ -39,12 +41,12 @@
 
 def relay(
     n_sec, lines, tokens, width, ff,
-    patches, cot, tab, wm, wd, gain, bias, bm, sv,
+    patches, cot, positions, counts, wm, wd, gain, bias, bm, sv,
     o_out, o_ig, o_w, o_d, o_small,
-    hin, gin, act, big1, big2, big3, wv, dv, cs, tabs, hout, gout, perm, bqk, freq,
+    hin, gin, act, big1, big2, big3, wv, dv, cs, tab, tabs, hout, gout, perm, bqk, freq,
     mine, zin, pin, sib, tmp, sg, sg_sib, sg_one, sg_two,
-    w_sem, hin_r, gin_r, tab_r, hop_s, gop_s, ini_s, cot_r, wd_s, wd_r, out_r, ig_r,
-    sib_s, sib_r, low_s, mine_r, za_s, zin_r, pb_s, pin_r, fin_l, fin_s, fin_r, sg_s, sg_r,
+    w_sem, hin_r, gin_r, tab_r, hop_s, gop_s, ini_s, cot_r, wd_s, wd_r, det_s, det_r, out_r, ig_r,
+    sib_s, sib_r, low_s, mine_r, za_s, zin_r, pb_s, pin_r, fin_l, fin_s, fin_r, guest_r, pass_s, pass_r, sg_s, sg_r,
 ):
     s = lax.axis_index("section")
     d = lax.axis_index("dp")
@@ -56,7 +58,13 @@
     half = tokens // 2
     n_main = (width // 256) * (ff // width)
     n_low = (ff // 2) // 256
-    n_chunk = n_main + n_low
+    n_own = n_main + n_low
+    n_chunk = n_own + n_low
+    n_away = N_AWAY
+    limit = jnp.where(
+        s == 0, n_main, jnp.where(s == 1, n_own - n_away, jnp.where(s == last, n_chunk, n_own + n_away))
+    )
+    n_side = jnp.where(s == 1, n_low + n_away, jnp.where(s == last, n_low, 0))
     n_sub = N_SUB
     score_scale = HEAD_DIM ** (-0.5)
 
@@ -102,6 +110,9 @@
     peers = n_sec + len(spots)
     for near, across, inner, outer in spots:
         peers = peers + jnp.where(inner, 1, 0)
+    tab[...] = jnp.zeros_like(tab)
+    tab[0, 0:2, :] = positions[0].astype(F32)
+    tab[0, 2:3, :] = jnp.broadcast_to(counts[...].astype(F32), (1, tokens))
     pl.semaphore_wait(barrier, peers)
 
     tab_sends = []
@@ -123,7 +134,6 @@
     @pl.when(s == 0)
     def _():
         patch_own.start()
-        cot_out.start()
 
     @pl.when(s != 0)
     def _():
@@ -162,10 +172,23 @@
         rows = down_rows(1 - side, core, k)
         return remote(dv.at[rows], dv.at[rows], wd_s.at[3, k], wd_r.at[3, k], to_dp(other))
 
-    @pl.when(even)
-    def _():
-        for k in range(n_part):
+    n_direct = n_part // 2
+
+    def down_out(k):
+        to = hout.at[last, pl.ds((k - n_direct) * part, part)]
+        send = remote(wd.at[0, down_rows(side, core, k)], to, wd_s.at[0, k], det_r.at[k - n_direct], to_section(last - 1))
+        return send
+
+    def down_on(k):
+        held = hout.at[last, pl.ds((k - n_direct) * part, part)]
+        to = dv.at[down_rows(side, core, k)]
+        return remote(held, to, det_s.at[k - n_direct], wd_r.at[0, k], to_section(1))
+
+    @pl.when(s == 0)
+    def _():
+        for k in range(n_direct):
             down_send(k).start()
+            down_out(k + n_direct).start()
 
     def table(i):
         pltpu.make_async_copy(tab.at[0], tabs.at[i], tab_r.at[i]).wait()
@@ -213,12 +236,19 @@
 
     @pl.when(s == last - 1)
     def _():
+        for k in range(n_direct, n_part):
+            down_out(k).wait_recv()
+            down_on(k).start()
+        for k in range(n_part):
+            down_send(k).start()
         cot_out.wait_recv()
         cot_on.start()
+        for k in range(n_direct, n_part):
+            down_on(k).wait_send()
 
     @pl.when(odd)
     def _():
-        for k in range(n_part):
+        for k in [0, 2, 1, 3]:
             down_send(k).wait_recv()
             down_near(k).start()
             down_pass(k).start()
@@ -256,22 +286,25 @@
                 lo = which * width + g * GROUP
                 t = nn(a, wv[:, lo : lo + GROUP]) + bqk[0:1, lo : lo + GROUP]
                 t1, t2 = t[:, :128], t[:, 128:]
-                r = jnp.concatenate([t1 * cosine - t2 * sine, t1 * sine + t2 * cosine], axis=1).astype(BF)
+                r = jnp.concatenate([t1 * cosine - t2 * sine, t1 * sine + t2 * cosine], axis=1)
+                r = (r * score_scale if which == 0 else r).astype(BF)
                 big1[i, :, lo : lo + GROUP] = r
                 turned.append(r)
             lo = 2 * width + g * GROUP
             value = (nn(a, wv[:, lo : lo + GROUP]) + bm[:, lo : lo + GROUP]).astype(BF)
             big1[i, :, lo : lo + GROUP] = value
             query, key = turned
-            context = jnp.zeros((tokens, GROUP), F32)
+            weights = []
             for e in range(4):
-                scores = nt(jnp.where(q_masks[e], query, zero_low), key) * score_scale
+                scores = nt(jnp.where(q_masks[e], query, zero_low), key)
                 scores = jnp.where(keys_on, scores, -1e30)
                 top = jnp.max(scores, axis=-1, keepdims=True)
                 p = jnp.exp(scores - top)
                 p = (p * (1.0 / jnp.sum(p, axis=-1, keepdims=True))).astype(BF)
                 big2[i, :, (4 * g + e) * tokens : (4 * g + e + 1) * tokens] = p
-                context = jnp.where(v_masks[e], nn(p, value), context)
+                weights.append(p)
+            stacked = jnp.concatenate([jnp.where(v_masks[e], value, zero_low) for e in range(4)], axis=0)
+            context = nn(jnp.concatenate(weights, axis=1), stacked)
             lo = 3 * width + g * GROUP
             big1[i, :, lo : lo + GROUP] = context.astype(BF)
         branch = nn(big1[i, :, 3 * width :], wv[:, 3 * width :]) + bm[:, 3 * width :]
@@ -297,27 +330,30 @@
             key = big1[i, :, klo : klo + GROUP]
             value = big1[i, :, vlo : vlo + GROUP]
             dctx = dctx_all[:, g * GROUP : (g + 1) * GROUP]
-            dq = jnp.zeros((tokens, GROUP), F32)
-            dk = jnp.zeros((tokens, GROUP), F32)
-            dval = jnp.zeros((tokens, GROUP), F32)
+            clo = 3 * width + g * GROUP
+            both = dctx.astype(F32) * big1[i, :, clo : clo + GROUP].astype(F32)
+            d_stack, p_stack, gs_list = [], [], []
             for e in range(4):
                 d_e = jnp.where(v_masks[e], dctx, zero_low)
-                q_e = jnp.where(q_masks[e], query, zero_low)
                 gw = nt(d_e, value)
                 p_low = big2[i, :, (4 * g + e) * tokens : (4 * g + e + 1) * tokens]
-                p = p_low.astype(F32)
-                pg = p * gw
-                gs = (pg - p * jnp.sum(pg, axis=-1, keepdims=True)).astype(BF)
-                dq = jnp.where(q_masks[e], nn(gs, key), dq)
-                dk = dk + tn(gs, q_e)
-                dval = dval + tn(p_low, d_e)
+                inside = jnp.sum(jnp.where(v_masks[e], both, 0.0), axis=-1, keepdims=True)
+                gs_list.append((p_low.astype(F32) * (gw - inside)).astype(BF))
+                d_stack.append(d_e)
+                p_stack.append(p_low)
+            key_low = key * jnp.asarray(score_scale, BF)
+            k_stack = jnp.concatenate([jnp.where(q_masks[e], key_low, zero_low) for e in range(4)], axis=0)
+            q_stack = jnp.concatenate([jnp.where(q_masks[e], query, zero_low) for e in range(4)], axis=0)
+            dq = nn(jnp.concatenate(gs_list, axis=1), k_stack)
+            dk = tn(jnp.concatenate(gs_list, axis=0), q_stack)
+            dval = tn(jnp.concatenate(p_stack, axis=0), jnp.concatenate(d_stack, axis=0))
             cosine = cs[i, 0, :, g * pairs : (g + 1) * pairs]
             sine = cs[i, 1, :, g * pairs : (g + 1) * pairs]
             turn = jnp.zeros((tokens, pairs), F32)
-            for lo, grad, held in ((qlo, dq, query), (klo, dk, key)):
-                g1, g2 = grad[:, :128] * score_scale, grad[:, 128:] * score_scale
+            for lo, grad, held, size in ((qlo, dq, query, 1.0 / score_scale), (klo, dk, key, 1.0)):
+                g1, g2 = grad[:, :128], grad[:, 128:]
                 r = held.astype(F32)
-                turn = turn + g2 * r[:, :128] - g1 * r[:, 128:]
+                turn = turn + (g2 * r[:, :128] - g1 * r[:, 128:]) * size
                 raw = jnp.concatenate([g1 * cosine + g2 * sine, g2 * cosine - g1 * sine], axis=1).astype(BF)
                 big3[i, :, lo : lo + GROUP] = raw
                 row = 3 if lo < width else 4
@@ -456,6 +492,10 @@
         def _():
             forward(i)
 
+        @pl.when((s == 0) & (j == 0))
+        def _():
+            cot_out.start()
+
         @pl.when(ahead & (j == 0))
         def _():
             lax.fori_loop(1, n_sec, lambda i, carry: (table(i), carry)[1], 0)
@@ -485,40 +525,69 @@
 
     my_half = pl.ds(core * n_sub, n_sub)
     their_half = pl.ds((1 - core) * n_sub, n_sub)
-    shift = jnp.where(odd, n_low, 0)
+
+    def is_own(c):
+        after = ((s == 1) & (c >= n_main) & (c < n_own - n_away)) | ((s == last) & (c >= n_own) & (c < n_chunk))
+        return ((c >= 0) & (c < n_main)) | after
+
+    def is_guest(c):
+        return ((s >= 2) & (c >= n_main) & (c < n_own)) | ((s == last - 1) & (c >= n_own) & (c < n_own + n_away))
 
     def sib_slot(c):
-        return jnp.where(c < 0, n_chunk + n_low + c, c)
+        return jnp.where(c >= n_own, c - n_low, c)
 
     def sib_copy(c):
-        slot = lax.rem(c + n_low, 2)
+        slot = lax.rem(c, 2)
         at = sib_slot(c)
         return remote(tmp.at[slot, their_half], sib.at[at], sib_s.at[slot], sib_r.at[at], to_dp(other))
 
-    def low_copy(c):
-        at = c + n_low
+    def side_copy(b):
+        slot = 2 + lax.rem(b, 2)
+        at = n_own + b
+        return remote(tmp.at[slot, their_half], sib.at[at], sib_s.at[slot], sib_r.at[at], to_dp(other))
+
+    def side_send(b):
+        to = jnp.where((s == 1) & (b < n_low), last, last - 1)
         return remote(
-            sib.at[n_chunk + at],
-            mine.at[pl.ds((n_main + at) * n_sub, n_sub)],
-            low_s.at[at],
-            mine_r.at[at],
-            to_section(lax.rem(s + last, n_sec)),
+            sib.at[n_own + b], mine.at[pl.ds((n_main + b) * n_sub, n_sub)], low_s.at[b], mine_r.at[b], to_section(to)
         )
 
+    def make_down(slot, row):
+        rows = pl.ds(pl.multiple_of(row, 256), 256)
+        left = big1[:, :, rows].reshape(n_sec * tokens, 256)
+        right = gin[...].reshape(n_sec * tokens, width)
+        keep(slot, tn(left, right))
+
+    def keep(slot, block):
+        tmp[slot] = block.astype(BF).reshape(2 * n_sub, half // n_sub, width)
+
+    def make_side(b):
+        slot = 2 + lax.rem(b, 2)
+
+        @pl.when(b >= 2)
+        def _():
+            side_copy(b - 2).wait_send()
+
+        make_down(slot, jnp.where(b < n_low, b, b + n_low - n_away) * 256)
+        side_copy(b).start()
+
+    def send_side(b):
+        slot = 2 + lax.rem(b, 2)
+        at = n_own + b
+        side_copy(b).wait_recv()
+        sib[at] = (tmp[slot, my_half].astype(F32) + sib[at].astype(F32)).astype(BF)
+        side_send(b).start()
+
     def make_block(c):
-        slot = lax.rem(c + n_low, 2)
-
-        @pl.when((even & (c >= 2)) | (odd & (c >= 2 - n_low)))
+        slot = lax.rem(c, 2)
+
+        @pl.when(c >= 2)
         def _():
             sib_copy(c - 2).wait_send()
 
         column = lax.rem(c, ff // width)
         row = c // (ff // width)
-        is_main = (c >= 0) & (c < n_main)
-        from_act = is_main & (odd | (column < 3))
-
-        def keep(block):
-            tmp[slot] = block.astype(BF).reshape(2 * n_sub, half // n_sub, width)
+        from_act = (c < n_main) & (odd | (column < 3))
 
         @pl.when(from_act)
         def _():
@@ -526,33 +595,31 @@
             columns = pl.ds(pl.multiple_of(column * width, width), width)
             left = act[:, :, rows].reshape(n_sec * tokens, 256)
             right = big3[:, :, columns].reshape(n_sec * tokens, width)
-            keep(tn(left, right))
+            keep(slot, tn(left, right))
 
         @pl.when(from_act & even & (column < 2))
         def _():
             back = perm[...]
             held = tmp[slot].reshape(2 * half, width)
             keep(
+                slot,
                 jnp.concatenate(
                     [nt(held[:, k * GROUP : (k + 1) * GROUP], back) for k in range(width // GROUP)], axis=1
-                )
+                ),
             )
 
         @pl.when(jnp.logical_not(from_act))
         def _():
-            down_row = jnp.where(c < 0, (c + n_low) * 256, ff // 2 + (c - n_main) * 256)
-            start = jnp.where(even, 3 * width + row * 256, down_row)
-            rows = pl.ds(pl.multiple_of(start, 256), 256)
-            left = big1[:, :, rows].reshape(n_sec * tokens, 256)
-            right = gin[...].reshape(n_sec * tokens, width)
-            keep(tn(left, right))
+            upper = ff // 2 + jnp.where(s == last, c - n_own, c - n_main) * 256
+            make_down(slot, jnp.where(even, 3 * width + row * 256, upper))
 
         sib_copy(c).start()
 
     def spot_copies(k, u):
         near, across, inner, outer = spots[k]
-        to_near = remote(mine.at[u], zin.at[k, u], za_s.at[k, u], zin_r.at[k, u], to_dp(near))
-        to_across = remote(zin.at[k, u], pin.at[k, u], pb_s.at[k, u], pin_r.at[k, u], to_dp(across))
+        held = lax.rem(u, SLOTS)
+        to_near = remote(mine.at[u], zin.at[k, held], za_s.at[k, u], zin_r.at[k, u], to_dp(near))
+        to_across = remote(zin.at[k, held], pin.at[k, held], pb_s.at[k, u], pin_r.at[k, u], to_dp(across))
         return to_near, to_across
 
     piece_rows = half // n_sub
@@ -566,16 +633,40 @@
         columns = pl.ds(pl.multiple_of(column * width, width), width)
         return o_w.at[rows, columns]
 
+    def d_rows(block, sub):
+        start = block * 256 + core * half + sub * piece_rows
+        return o_d.at[pl.ds(pl.multiple_of(start, piece_rows), piece_rows), :]
+
     def d_place(u):
         c = u // n_sub
-        start = (c - n_main) * 256 + core * half + lax.rem(u, n_sub) * piece_rows
-        return o_d.at[pl.ds(pl.multiple_of(start, piece_rows), piece_rows), :]
+        late = jnp.where(s == last, c - n_own, c - n_own + n_low - n_away)
+        return d_rows(jnp.where(c < n_own, c - n_main, late), lax.rem(u, n_sub))
 
     def finish_copies(u, place):
         here = pltpu.make_async_copy(mine.at[u], place, fin_l.at[u])
         there = remote(mine.at[u], place, fin_s.at[u], fin_r.at[u], to_dp(other))
         return here, there
 
+    def is_away(u):
+        return ((s == last) & (u < n_own * n_sub)) | ((s == last - 1) & (u >= n_own * n_sub))
+
+    def guest_send(u):
+        at = jnp.where(s == last, u - n_main * n_sub, u - n_own * n_sub)
+        to = jnp.where(s == last, 0, 1)
+        return remote(mine.at[u], d_place(u), fin_s.at[u], guest_r.at[at], to_section(to))
+
+    def returned(g):
+        block = g // n_sub + jnp.where(s == 0, 0, n_low - n_away)
+        return d_rows(block, lax.rem(g, n_sub))
+
+    def guest_take(g):
+        return remote(mine.at[0], returned(g), pass_s.at[g], guest_r.at[g], to_dp(other))
+
+    def guest_pass(g):
+        return remote(returned(g), returned(g), pass_s.at[g], pass_r.at[g], to_dp(other))
+
+    n_returned = jnp.where(s == 0, n_low * n_sub, jnp.where(s == 1, n_away * n_sub, 0))
+
     def finish(u):
         @pl.when(u < n_main * n_sub)
         def _():
@@ -583,11 +674,15 @@
             here.start()
             there.start()
 
-        @pl.when(u >= n_main * n_sub)
+        @pl.when((u >= n_main * n_sub) & jnp.logical_not(is_away(u)))
         def _():
             here, there = finish_copies(u, d_place(u))
             here.start()
             there.start()
+
+        @pl.when((u >= n_main * n_sub) & is_away(u))
+        def _():
+            guest_send(u).start()
 
     small_sib = remote(sg, sg_sib, sg_s.at[0], sg_r.at[0], to_dp(other))
 
@@ -598,38 +693,38 @@
         return to_near, to_across
 
     n_unit = n_chunk * n_sub
-    steps = n_unit + n_low * n_sub + n_sub * LAG_SIB + len(lines) * LAG_END + 1
+    my_units = limit * n_sub
+    steps = my_units + n_sub * LAG_SIB + len(lines) * LAG_END + 1
 
     def sum_step(t, carry):
-        v = t - shift * n_sub
-        c = v // n_sub
-
-        @pl.when((lax.rem(t, n_sub) == 0) & ((even & (c < n_main)) | (odd & (c < n_chunk))))
-        def _():
-            make_block(t // n_sub - shift)
-
-        c1 = t // n_sub - shift - LAG_SIB
+        c = t // n_sub
         first = lax.rem(t, n_sub) == 0
-
-        @pl.when(first & ((even & (c1 >= 0) & (c1 < n_main)) | (odd & (c1 >= -n_low) & (c1 < n_chunk))))
-        def _():
-            slot = lax.rem(c1 + n_low, 2)
+        second = lax.rem(t, n_sub) == 1
+
+        @pl.when(first & is_own(c))
+        def _():
+            make_block(c)
+
+        @pl.when(second & (c < n_side))
+        def _():
+            make_side(c)
+
+        c1 = c - LAG_SIB
+
+        @pl.when(first & is_own(c1))
+        def _():
+            slot = lax.rem(c1, 2)
             at = sib_slot(c1)
             sib_copy(c1).wait_recv()
-            total = (tmp[slot, my_half].astype(F32) + sib[at].astype(F32)).astype(BF)
-
-            @pl.when(c1 < 0)
-            def _():
-                sib[at] = total
-                low_copy(c1).start()
-
-            @pl.when(c1 >= 0)
-            def _():
-                mine[pl.ds(c1 * n_sub, n_sub)] = total
-
-        @pl.when(first & even & (c1 >= n_main) & (c1 < n_chunk))
-        def _():
-            low_copy(c1 - n_chunk).wait_recv()
+            mine[pl.ds(c1 * n_sub, n_sub)] = (tmp[slot, my_half].astype(F32) + sib[at].astype(F32)).astype(BF)
+
+        @pl.when(second & (c1 >= 0) & (c1 < n_side))
+        def _():
+            send_side(c1)
+
+        @pl.when(first & is_guest(c1))
+        def _():
+            side_send(c1 - n_main).wait_recv()
 
         @pl.when(t == 0)
         def _():
@@ -670,46 +765,55 @@
         for k in range(len(lines)):
             near, across, inner, outer = spots[k]
             base = LAG_SIB * n_sub + k * LAG_END
-            u0 = v - base
-
-            @pl.when(outer & (u0 >= 0) & (u0 < n_unit))
+            u0 = t - base
+
+            @pl.when(outer & (u0 >= 0) & (u0 < my_units))
             def _():
                 to_near, _ = spot_copies(k, u0)
                 to_near.start()
 
-            u2 = v - base - LAG_ONE
-
-            @pl.when(inner & (u2 >= 0) & (u2 < n_unit))
+            u2 = t - base - LAG_ONE
+
+            @pl.when(inner & (u2 >= 0) & (u2 < my_units))
             def _():
                 to_near, to_across = spot_copies(k, u2)
                 to_near.wait_recv()
-                zin[k, u2] = (mine[u2].astype(F32) + zin[k, u2].astype(F32)).astype(BF)
+                held = lax.rem(u2, SLOTS)
+                zin[k, held] = (mine[u2].astype(F32) + zin[k, held].astype(F32)).astype(BF)
                 to_across.start()
 
-            u3 = v - base - LAG_TWO
-
-            @pl.when(inner & (u3 >= 0) & (u3 < n_unit))
+            u3 = t - base - LAG_TWO
+
+            @pl.when(inner & (u3 >= 0) & (u3 < my_units))
             def _():
                 to_near, to_across = spot_copies(k, u3)
-                to_across.wait_recv()
-                mine[u3] = (zin[k, u3].astype(F32) + pin[k, u3].astype(F32)).astype(BF)
+                to_across.wait()
+                held = lax.rem(u3, SLOTS)
+                mine[u3] = (zin[k, held].astype(F32) + pin[k, held].astype(F32)).astype(BF)
                 to_near.start()
                 if k == len(lines) - 1:
                     finish(u3)
 
-            u4 = v - base - LAG_END
-
-            @pl.when(outer & (u4 >= 0) & (u4 < n_unit))
+            u4 = t - base - LAG_END
+
+            @pl.when(outer & (u4 >= 0) & (u4 < my_units))
             def _():
                 to_near, _ = spot_copies(k, u4)
                 to_near.wait()
-                mine[u4] = zin[k, u4]
+                mine[u4] = zin[k, lax.rem(u4, SLOTS)]
                 if k == len(lines) - 1:
                     finish(u4)
 
         return carry
 
     lax.fori_loop(0, steps, sum_step, 0)
+
+    def take(g, carry):
+        guest_take(g).wait_recv()
+        guest_pass(g).start()
+        return carry
+
+    lax.fori_loop(0, n_returned, take, 0)
     o_small[...] = sg[...]
 
     for send in tab_sends:
@@ -727,8 +831,9 @@
     def _():
         for k in range(n_part):
             down_send(k).wait_send()
-        sib_copy(n_main - 2).wait_send()
-        sib_copy(n_main - 1).wait_send()
+
+    sib_copy(0).wait_send()
+    sib_copy(1).wait_send()
 
     @pl.when(odd)
     def _():
@@ -736,10 +841,15 @@
             down_near(k).wait_send()
             down_pass(k).wait_send()
             down_pass_far(k).wait_send()
-        sib_copy(n_chunk - 2).wait_send()
-        sib_copy(n_chunk - 1).wait_send()
-        for c in range(-n_low, 0):
-            low_copy(c).wait_send()
+        side_copy(0).wait_send()
+        side_copy(1).wait_send()
+        for b in range(n_low):
+            side_send(b).wait_send()
+
+    @pl.when(s == 1)
+    def _():
+        for b in range(n_low, n_low + n_away):
+            side_send(b).wait_send()
 
     back_send(last, last % 2).wait_send()
 
@@ -764,12 +874,11 @@
         @pl.when(inner)
         def _():
             def drain(u, carry):
-                to_near, to_across = spot_copies(k, u)
+                to_near, _ = spot_copies(k, u)
                 to_near.wait_send()
-                to_across.wait_send()
                 return carry
 
-            lax.fori_loop(0, n_unit, drain, 0)
+            lax.fori_loop(0, my_units, drain, 0)
 
     def drain_main(u, carry):
         here, there = finish_copies(u, w_place(u))
@@ -783,8 +892,30 @@
         there.wait()
         return carry
 
+    def drain_guest(u, carry):
+        guest_send(u).wait_send()
+        return carry
+
+    def drain_pass(g, carry):
+        guest_pass(g).wait()
+        return carry
+
     lax.fori_loop(0, n_main * n_sub, drain_main, 0)
-    lax.fori_loop(n_main * n_sub, n_unit, drain_down, 0)
+    lax.fori_loop(0, n_returned, drain_pass, 0)
+
+    @pl.when(s == 1)
+    def _():
+        lax.fori_loop(n_main * n_sub, (n_own - n_away) * n_sub, drain_down, 0)
+
+    @pl.when(s == last - 1)
+    def _():
+        lax.fori_loop(n_main * n_sub, n_own * n_sub, drain_down, 0)
+        lax.fori_loop(n_own * n_sub, (n_own + n_away) * n_sub, drain_guest, 0)
+
+    @pl.when(s == last)
+    def _():
+        lax.fori_loop(n_main * n_sub, n_own * n_sub, drain_guest, 0)
+        lax.fori_loop(n_own * n_sub, n_unit, drain_down, 0)
 
 
 def line_strides(n_dp):
@@ -801,16 +932,9 @@
     ff = wm.shape[2]
     lines = line_strides(n_dp)
     n_low = (ff // 2) // 256
-    n_chunk = (width // 256) * (ff // width) + n_low
+    n_own = (width // 256) * (ff // width) + n_low
+    n_chunk = n_own + n_low
     n_unit, rows = n_chunk * N_SUB, 128 // N_SUB
-    tab = jnp.concatenate(
-        [
-            positions[0].astype(F32),
-            jnp.broadcast_to(counts.astype(F32)[:, None], (1, tokens)),
-            jnp.zeros((5, tokens), F32),
-        ],
-        axis=0,
-    )[None]
     any_spec = pl.BlockSpec(memory_space=pl.ANY)
     vmem_spec = pl.BlockSpec(memory_space=pltpu.VMEM)
     image = (n_sec, tokens, width)
@@ -827,6 +951,7 @@
         pltpu.VMEM((width, ff), BF),
         pltpu.VMEM((ff, width), BF),
         pltpu.VMEM((n_sec, 2, tokens, width // 2), F32),
+        pltpu.VMEM((1, 8, tokens), F32),
         pltpu.VMEM((n_sec, 8, tokens), F32),
         pltpu.VMEM(image, BF),
         pltpu.VMEM((2, tokens, width), BF),
@@ -834,10 +959,10 @@
         pltpu.VMEM((8, 2 * width), F32),
         pltpu.VMEM((8, width // 2), F32),
         pltpu.VMEM((n_unit, rows, width), BF),
-        pltpu.VMEM((n_line, n_unit, rows, width), BF),
-        pltpu.VMEM((n_line, n_unit, rows, width), BF),
-        pltpu.VMEM((n_chunk + n_low, N_SUB, rows, width), BF),
-        pltpu.VMEM((2, 2 * N_SUB, rows, width), BF),
+        pltpu.VMEM((n_line, SLOTS, rows, width), BF),
+        pltpu.VMEM((n_line, SLOTS, rows, width), BF),
+        pltpu.VMEM((n_own + n_low + N_AWAY, N_SUB, rows, width), BF),
+        pltpu.VMEM((4, 2 * N_SUB, rows, width), BF),
         pltpu.VMEM((8, width), F32),
         pltpu.VMEM((8, width), F32),
         pltpu.VMEM((n_line, 8, width), F32),
@@ -852,12 +977,14 @@
         dma,
         dma((4, 4)),
         dma((4, 4)),
+        dma((2,)),
+        dma((2,)),
         dma,
         dma,
-        dma((2,)),
-        dma((n_chunk + n_low,)),
-        dma((n_low,)),
-        dma((n_low,)),
+        dma((4,)),
+        dma((n_own + n_low + N_AWAY,)),
+        dma((n_low + N_AWAY,)),
+        dma((n_low + N_AWAY,)),
         dma((n_line, n_unit)),
         dma((n_line, n_unit)),
         dma((n_line, n_unit)),
@@ -865,6 +992,9 @@
         dma((n_unit,)),
         dma((n_unit,)),
         dma((n_unit,)),
+        dma((n_low * N_SUB,)),
+        dma((n_low * N_SUB,)),
+        dma((n_low * N_SUB,)),
         dma((1 + 2 * n_line,)),
         dma((1 + 2 * n_line,)),
     ]
@@ -877,13 +1007,13 @@
             jax.ShapeDtypeStruct((ff // 2, width), BF),
             jax.ShapeDtypeStruct((8, width), F32),
         ),
-        in_specs=[any_spec, any_spec, vmem_spec, any_spec, any_spec] + [vmem_spec] * 4,
+        in_specs=[any_spec] * 2 + [vmem_spec] * 2 + [any_spec] * 2 + [vmem_spec] * 4,
         out_specs=(any_spec, any_spec, any_spec, any_spec, vmem_spec),
         scratch_shapes=scratch,
         compiler_params=pltpu.CompilerParams(
             collective_id=0, has_side_effects=True, vmem_limit_bytes=63 * 2**20
         ),
-    )(patches, cot, tab, wm, wd, gain, bias, bm, sv)
+    )(patches, cot, positions, counts.reshape(1, 1), wm, wd, gain, bias, bm, sv)
     return (
         out,
         ig,

time: 260 us -> 240 us (0.923)
  the two profiles are of different devices: /device:TPU:0 before, /device:TPU:3 now
where the time goes in v3:
time: 240 us; the launch traced here: 239 us
  Pallas kernels  224 us (93%)
  other arithmetic  10.1 us (4%)
  local copies, waits for them, and re-layouts  4.3 us (2%)
    pallas_call x1, Pallas kernels, on_device(): pl.pallas_call(functools.partial(relay, n_sec, lines, tokens, width, ff),...  224 us
    broadcast_in_dim x1, other arithmetic, on_device(): gw.astype(F32)[None]  7.52 us

profile of v3, /device:TPU:3, one launch (start us, length us, event | category | flops | bytes accessed | tf_op | source)
XLA Modules:
  0.0 239.4 jit_solution(13806082789215908960)
XLA Ops:
  1.3 223.8 %shard_map.161 = (bf16[1,256,768]{2,1,0:T(8,128)(2,1)}, bf16[1,256,768]{2,1,0:T(8,128)(2,1)}, bf16[768,3072]{1,0:T(8,128)(2,1)}, bf16[1536,768]{1,0:T(8,128)(2,1)}, f32[8,768]{1,0:T(8,128)}) custom-call(bf16[1,256,768]{2,1,0:T(8,128)(2,1)} %patches.1, bf16[1,256,768]{2,1,0:T(8,128)(2,1)} %cot.1, s32[1,2,256]{2,1,0:T(2,128)} %positions.1, ...), custom_call_target="tpu_custom_call" | custom-call | tf_op jit(solution)/shard_map/pallas_call | solution.py:1001
  225.1 1.4 fusion
  226.5 0.7 slice_bitcast_fusion
  227.3 0.6 copy.18
  227.9 0.0 copy-start
  227.9 7.5 %bitcast_convert_fusion = f32[1,768,3072]{2,1,0:T(8,128)} fusion(bf16[768,3072]{1,0:T(8,128)(2,1)} %get-tuple-element.16), kind=kLoop, calls=%fused_computation | loop fusion | flops 2359296 | bytes 14155776 | tf_op jit(solution)/shard_map/broadcast_in_dim | solution.py:1022
  235.4 0.0 copy-start.2
  235.4 0.0 copy-start.1
  235.4 0.0 copy-done
  235.4 2.5 %bitcast_convert_fusion.1 = f32[1,1536,768]{2,1,0:T(8,128)} fusion(bf16[1536,768]{1,0:T(8,128)(2,1)S(1)} %copy-done), kind=kLoop, calls=%fused_computation.1 | loop fusion | flops 1179648 | bytes 7077888 | tf_op jit(solution)/shard_map/broadcast_in_dim | solution.py:1025
  237.9 0.0 copy-done.2
  237.9 0.7 copy.22
  238.7 0.0 copy-done.1
  238.7 0.7 copy.23
Async XLA Ops:
  227.9 7.5 %copy-start = (bf16[1536,768]{1,0:T(8,128)(2,1)S(1)}, bf16[1536,768]{1,0:T(8,128)(2,1)}, u32[]{:S(2)}) copy-start(bf16[1536,768]{1,0:T(8,128)(2,1)} %get-tuple-element.17) | copy-start | bytes 7077892
  235.4 2.6 %copy-start.2 = (bf16[1,256,768]{2,1,0:T(8,128)(2,1)S(1)}, bf16[1,256,768]{2,1,0:T(8,128)(2,1)}, u32[]{:S(2)}) copy-start(bf16[1,256,768]{2,1,0:T(8,128)(2,1)} %get-tuple-element.29) | copy-start | bytes 1179652
  235.4 3.3 %copy-start.1 = (bf16[1,256,768]{2,1,0:T(8,128)(2,1)S(1)}, bf16[1,256,768]{2,1,0:T(8,128)(2,1)}, u32[]{:S(2)}) copy-start(bf16[1,256,768]{2,1,0:T(8,128)(2,1)} %get-tuple-element.30) | copy-start | bytes 1179652

commit v4 on v3

--- a/solution.py
+++ b/solution.py
@@ -18,7 +18,7 @@
 LAG_SIB, LAG_ONE, LAG_TWO, LAG_END = 1, 2, 4, 6
 N_SUB = 2
 SLOTS = 8
-N_AWAY = 3
+N_AWAY = 1
 
 
 def nn(a, b, precision=None):
@@ -124,28 +124,50 @@
         send.start()
     tab_own = pltpu.make_async_copy(tab.at[0], tabs.at[s], tab_r.at[s])
     tab_own.start()
-    patch_send = remote(patches.at[0], hin.at[s], ini_s.at[n_sec], hin_r.at[s], to_section(0))
-    patch_own = pltpu.make_async_copy(patches.at[0], hin.at[0], hin_r.at[0])
-    cot_send = remote(cot.at[0], gin.at[s], ini_s.at[n_sec + 1], gin_r.at[s], to_section(last))
-    cot_own = pltpu.make_async_copy(cot.at[0], gin.at[last], gin_r.at[last])
-    cot_out = remote(cot.at[0], gout.at[0], ini_s.at[n_sec + 1], cot_r, to_section(last - 1))
-    cot_on = remote(gout.at[0], gin.at[0], ini_s.at[n_sec + 2], gin_r.at[0], to_section(last))
+    def rows_of(h):
+        return pl.ds(h * half, half)
+
+    def patch_send(h):
+        r = rows_of(h)
+        return remote(patches.at[0, r], hin.at[s, r], ini_s.at[n_sec + h], hin_r.at[s, h], to_section(0))
+
+    def patch_own(h):
+        r = rows_of(h)
+        return pltpu.make_async_copy(patches.at[0, r], hin.at[0, r], hin_r.at[0, h])
+
+    def cot_send(h):
+        r = rows_of(h)
+        return remote(cot.at[0, r], gin.at[s, r], ini_s.at[n_sec + 2 + h], gin_r.at[s, h], to_section(last))
+
+    def cot_own(h):
+        r = rows_of(h)
+        return pltpu.make_async_copy(cot.at[0, r], gin.at[last, r], gin_r.at[last, h])
+
+    cot_out = remote(cot.at[0], gout.at[0], ini_s.at[n_sec + 2], cot_r, to_section(last - 1))
+
+    def cot_on(h):
+        r = rows_of(h)
+        return remote(gout.at[0, r], gin.at[0, r], ini_s.at[n_sec + 4 + h], gin_r.at[0, h], to_section(last))
 
     @pl.when(s == 0)
     def _():
-        patch_own.start()
+        for h in range(2):
+            patch_own(h).start()
 
     @pl.when(s != 0)
     def _():
-        patch_send.start()
+        for h in range(2):
+            patch_send(h).start()
 
     @pl.when((s != 0) & (s != last))
     def _():
-        cot_send.start()
+        for h in range(2):
+            cot_send(h).start()
 
     @pl.when(s == last)
     def _():
-        cot_own.start()
+        for h in range(2):
+            cot_own(h).start()
 
     near0 = spots[0][0]
     side = lax.rem(d // lines[0], 2)
@@ -242,7 +264,8 @@
         for k in range(n_part):
             down_send(k).start()
         cot_out.wait_recv()
-        cot_on.start()
+        for h in range(2):
+            cot_on(h).start()
         for k in range(n_direct, n_part):
             down_on(k).wait_send()
 
@@ -310,8 +333,8 @@
         branch = nn(big1[i, :, 3 * width :], wv[:, 3 * width :]) + bm[:, 3 * width :]
         hout[slot] = (x + row_mask(i) * branch).astype(BF)
 
-    def norm_backward(i, g_up, gact):
-        xhat, scale = normalise(hin[i].astype(F32))
+    def norm_backward(x, g_up, gact):
+        xhat, scale = normalise(x.astype(F32))
         sg[0:1, :] += jnp.sum(gact * xhat, axis=0, keepdims=True)
         sg[1:2, :] += jnp.sum(gact, axis=0, keepdims=True)
         gn = gact * gain[...]
@@ -368,24 +391,12 @@
             at = width // 2 + g * pairs
             sg[2:3, at : at + pairs] += sums[1:2]
         gact = nt(big3[i, :, : 3 * width], wv[:, : 3 * width])
-        gout[slot] = norm_backward(i, g_up, gact).astype(BF)
+        gout[slot] = norm_backward(hin[i], g_up, gact).astype(BF)
         gin[i] = low
 
     piece = 512
 
-    def dense_forward(i, slot):
-        x = hin[i].astype(F32)
-        xhat, _ = normalise(x)
-        a = (xhat * gain[...] + bias[...]).astype(BF)
-        act[i] = a
-        for k in range(ff // piece):
-            lo = k * piece
-            pre = nn(a, wv[:, lo : lo + piece]) + bm[:, lo : lo + piece]
-            cdf = 0.5 + 0.5 * lax.erf(pre * (0.5**0.5))
-            big1[i, :, lo : lo + piece] = (pre * cdf).astype(BF)
-            pdf = jnp.exp(-0.5 * (pre * pre)) * 0.3989422804014327
-            big2[i, :, lo : lo + piece] = (cdf + pre * pdf).astype(BF)
-
+    def down_ready(i):
         @pl.when(i == 0)
         def _():
             load_d.wait()
@@ -396,8 +407,23 @@
                 down_pass(k).wait_recv()
                 down_pass_far(k).wait_recv()
 
-        branch = nn(big1[i], dv[...]) + sv[...]
-        hout[slot] = (x + row_mask(i) * branch).astype(BF)
+    def dense_forward(i, h):
+        r = slice(h * half, (h + 1) * half)
+        x = hin[i, r].astype(F32)
+        xhat, _ = normalise(x)
+        a = (xhat * gain[...] + bias[...]).astype(BF)
+        act[i, r] = a
+        for k in range(ff // piece):
+            lo = k * piece
+            pre = nn(a, wv[:, lo : lo + piece]) + bm[:, lo : lo + piece]
+            cdf = 0.5 + 0.5 * lax.erf(pre * (0.5**0.5))
+            big1[i, r, lo : lo + piece] = (pre * cdf).astype(BF)
+            pdf = jnp.exp(-0.5 * (pre * pre)) * 0.3989422804014327
+            big2[i, r, lo : lo + piece] = (cdf + pre * pdf).astype(BF)
+        if h == 0:
+            down_ready(i)
+        branch = nn(big1[i, r], dv[...]) + sv[...]
+        hout[i, r] = (x + row_mask(i)[r] * branch).astype(BF)
 
     def dense_backward(i, slot):
         g_up = gin[i].astype(F32)
@@ -413,68 +439,90 @@
                 at = m * GROUP
                 sg[3 + k : 4 + k, at : at + GROUP] += jnp.sum(gpre.astype(F32), axis=0, keepdims=True)
         gact = nt(big3[i], wv[...])
-        gout[slot] = norm_backward(i, g_up, gact).astype(BF)
+        gout[slot] = norm_backward(hin[i], g_up, gact).astype(BF)
         gin[i] = low
 
-    def hop_send(i, slot):
-        return remote(hout.at[slot], hin.at[i], hop_s.at[i], hin_r.at[i], to_section(lax.rem(s + 1, n_sec)))
-
-    def result_send(i, slot):
-        return remote(hout.at[slot], o_out.at[0], hop_s.at[i], out_r, to_section(i))
-
-    def back_send(i, slot):
-        return remote(gout.at[slot], gin.at[i], gop_s.at[i], gin_r.at[i], to_section(lax.rem(s + last, n_sec)))
+    def hop_send(i, h):
+        r = rows_of(h)
+        to = to_section(lax.rem(s + 1, n_sec))
+        return remote(hout.at[i, r], hin.at[i, r], hop_s.at[i, h], hin_r.at[i, h], to)
+
+    def result_send(i):
+        return remote(hout.at[i], o_out.at[0], hop_s.at[i, 0], out_r, to_section(i))
+
+    def back_send(i, slot, h):
+        r = rows_of(h)
+        to = to_section(lax.rem(s + last, n_sec))
+        return remote(gout.at[slot, r], gin.at[i, r], gop_s.at[i, h], gin_r.at[i, h], to)
 
     def input_send(i, slot):
-        return remote(gout.at[slot], o_ig.at[0], gop_s.at[i], ig_r, to_section(i))
+        return remote(gout.at[slot], o_ig.at[0], gop_s.at[i, 0], ig_r, to_section(i))
+
+    def send_hop(i, h):
+        @pl.when((s != last) & (i >= 1))
+        def _():
+            hop_send(i - 1, h).wait_send()
+
+        @pl.when(s != last)
+        def _():
+            hop_send(i, h).start()
+
+    def send_back(i, slot, h):
+        @pl.when((s != 0) & (i >= 1))
+        def _():
+            back_send(i - 1, 1 - slot, h).wait_send()
+
+        @pl.when(s != 0)
+        def _():
+            back_send(i, slot, h).start()
 
     def forward(i):
-        hop_send(i, i).wait_recv()
-
         @pl.when(even)
         def _():
+            for h in range(2):
+                hop_send(i, h).wait_recv()
             attention_forward(i, i)
+            for h in range(2):
+                send_hop(i, h)
 
         @pl.when(odd)
         def _():
-            dense_forward(i, i)
-
-        @pl.when((s != last) & (i >= 1))
-        def _():
-            hop_send(i - 1, i - 1).wait_send()
-
-        @pl.when(s != last)
-        def _():
-            hop_send(i, i).start()
+            for h in range(2):
+                hop_send(i, h).wait_recv()
+                dense_forward(i, h)
+                send_hop(i, h)
 
     def backward(i):
         slot = lax.rem(i, 2)
 
         @pl.when((i == 0) & (s == last - 1))
         def _():
-            cot_on.wait_send()
+            for h in range(2):
+                cot_on(h).wait_send()
 
         @pl.when((i == 2) & (s == 0))
         def _():
             pltpu.make_async_copy(gout.at[slot], o_ig.at[0], ig_r).wait()
 
-        back_send(i, slot).wait_recv()
-
         @pl.when(even)
         def _():
+            for h in range(2):
+                back_send(i, slot, h).wait_recv()
             attention_backward(i, slot)
+            for h in range(2):
+                send_back(i, slot, h)
 
         @pl.when(odd)
         def _():
+            for h in range(2):
+                back_send(i, slot, h).wait_recv()
             dense_backward(i, slot)
-
-        @pl.when((i >= 2) | ((i == 1) & (s != 0)))
-        def _():
-            back_send(i - 1, 1 - slot).wait_send()
-
-        @pl.when(s != 0)
-        def _():
-            back_send(i, slot).start()
+            for h in range(2):
+                send_back(i, slot, h)
+
+        @pl.when((s == 0) & (i >= 2))
+        def _():
+            input_send(i - 1, 1 - slot).wait_send()
 
         @pl.when((s == 0) & (i != 0))
         def _():
@@ -511,7 +559,7 @@
     @pl.when(s == last)
     def _():
         for i in range(last):
-            result_send(i, i).start()
+            result_send(i).start()
         pltpu.make_async_copy(hout.at[last], o_out.at[0], out_r).start()
 
     @pl.when(even)
@@ -821,11 +869,17 @@
 
     @pl.when(s != 0)
     def _():
-        patch_send.wait_send()
-
-    @pl.when(s != last)
-    def _():
-        cot_send.wait_send()
+        for h in range(2):
+            patch_send(h).wait_send()
+
+    @pl.when(s == 0)
+    def _():
+        cot_out.wait_send()
+
+    @pl.when((s != 0) & (s != last))
+    def _():
+        for h in range(2):
+            cot_send(h).wait_send()
 
     @pl.when(even)
     def _():
@@ -851,16 +905,24 @@
         for b in range(n_low, n_low + n_away):
             side_send(b).wait_send()
 
-    back_send(last, last % 2).wait_send()
+    @pl.when(s == 0)
+    def _():
+        input_send(last, last % 2).wait_send()
+
+    @pl.when(s != 0)
+    def _():
+        for h in range(2):
+            back_send(last, last % 2, h).wait_send()
 
     @pl.when(s != last)
     def _():
-        hop_send(last, last).wait_send()
+        for h in range(2):
+            hop_send(last, h).wait_send()
 
     @pl.when(s == last)
     def _():
         for i in range(last):
-            result_send(i, i).wait_send()
+            result_send(i).wait_send()
 
     pltpu.make_async_copy(hout.at[0], o_out.at[0], out_r).wait()
 
@@ -968,12 +1030,12 @@
         pltpu.VMEM((n_line, 8, width), F32),
         pltpu.VMEM((n_line, 8, width), F32),
         dma((2,)),
+        dma((n_sec, 2)),
+        dma((n_sec, 2)),
         dma((n_sec,)),
-        dma((n_sec,)),
-        dma((n_sec,)),
-        dma((n_sec,)),
-        dma((n_sec,)),
-        dma((n_sec + 3,)),
+        dma((n_sec, 2)),
+        dma((n_sec, 2)),
+        dma((n_sec + 6,)),
         dma,
         dma((4, 4)),
         dma((4, 4)),

time: 240 us -> 228 us (0.950)
  the two profiles are of different devices: /device:TPU:3 before, /device:TPU:0 now
where the time goes in v4:
time: 228 us; the launch traced here: 225 us
  Pallas kernels  209 us (92%)
  other arithmetic  10.1 us (4%)
  local copies, waits for them, and re-layouts  4.3 us (2%)
    pallas_call x1, Pallas kernels, on_device(): pl.pallas_call(functools.partial(relay, n_sec, lines, tokens, width, ff),...  209 us
    broadcast_in_dim x1, other arithmetic, on_device(): gw.astype(F32)[None]  7.52 us

profile of v4, /device:TPU:0, one launch (start us, length us, event | category | flops | bytes accessed | tf_op | source)
XLA Modules:
  0.0 224.7 jit_solution(15990956295185594327)
XLA Ops:
  1.3 209.1 %shard_map.161 = (bf16[1,256,768]{2,1,0:T(8,128)(2,1)}, bf16[1,256,768]{2,1,0:T(8,128)(2,1)}, bf16[768,3072]{1,0:T(8,128)(2,1)}, bf16[1536,768]{1,0:T(8,128)(2,1)}, f32[8,768]{1,0:T(8,128)}) custom-call(bf16[1,256,768]{2,1,0:T(8,128)(2,1)} %patches.1, bf16[1,256,768]{2,1,0:T(8,128)(2,1)} %cot.1, s32[1,2,256]{2,1,0:T(2,128)} %positions.1, ...), custom_call_target="tpu_custom_call" | custom-call | tf_op jit(solution)/shard_map/pallas_call | solution.py:1063
  210.3 1.4 fusion
  211.8 0.7 slice_bitcast_fusion
  212.5 0.6 copy.18
  213.1 0.0 copy-start
  213.1 7.5 %bitcast_convert_fusion = f32[1,768,3072]{2,1,0:T(8,128)} fusion(bf16[768,3072]{1,0:T(8,128)(2,1)} %get-tuple-element.16), kind=kLoop, calls=%fused_computation | loop fusion | flops 2359296 | bytes 14155776 | tf_op jit(solution)/shard_map/broadcast_in_dim | solution.py:1084
  220.7 0.0 copy-start.2
  220.7 0.0 copy-start.1
  220.7 0.0 copy-done
  220.7 2.5 %bitcast_convert_fusion.1 = f32[1,1536,768]{2,1,0:T(8,128)} fusion(bf16[1536,768]{1,0:T(8,128)(2,1)S(1)} %copy-done), kind=kLoop, calls=%fused_computation.1 | loop fusion | flops 1179648 | bytes 7077888 | tf_op jit(solution)/shard_map/broadcast_in_dim | solution.py:1087
  223.2 0.0 copy-done.2
  223.2 0.7 copy.22
  224.0 0.0 copy-done.1
  224.0 0.7 copy.23
Async XLA Ops:
  213.1 7.5 %copy-start = (bf16[1536,768]{1,0:T(8,128)(2,1)S(1)}, bf16[1536,768]{1,0:T(8,128)(2,1)}, u32[]{:S(2)}) copy-start(bf16[1536,768]{1,0:T(8,128)(2,1)} %get-tuple-element.17) | copy-start | bytes 7077892
  220.7 2.6 %copy-start.2 = (bf16[1,256,768]{2,1,0:T(8,128)(2,1)S(1)}, bf16[1,256,768]{2,1,0:T(8,128)(2,1)}, u32[]{:S(2)}) copy-start(bf16[1,256,768]{2,1,0:T(8,128)(2,1)} %get-tuple-element.29) | copy-start | bytes 1179652
  220.7 3.3 %copy-start.1 = (bf16[1,256,768]{2,1,0:T(8,128)(2,1)S(1)}, bf16[1,256,768]{2,1,0:T(8,128)(2,1)}, u32[]{:S(2)}) copy-start(bf16[1,256,768]{2,1,0:T(8,128)(2,1)} %get-tuple-element.30) | copy-start | bytes 1179652

commit v5 on v4

--- a/solution.py
+++ b/solution.py
@@ -212,6 +212,14 @@
             down_send(k).start()
             down_out(k + n_direct).start()
 
+    @pl.when(s == last - 1)
+    def _():
+        for k in range(n_direct, n_part):
+            down_out(k).wait_recv()
+            down_on(k).start()
+        for k in range(n_part):
+            down_send(k).start()
+
     def table(i):
         pltpu.make_async_copy(tab.at[0], tabs.at[i], tab_r.at[i]).wait()
         angle = nn(jnp.transpose(tabs[i]), freq[...], HI)
@@ -241,7 +249,6 @@
             pltpu.make_async_copy(tab.at[0], tabs.at[i], tab_r.at[i]).wait()
 
     sg[...] = jnp.zeros_like(sg)
-    load_w.wait()
 
     @pl.when(even)
     def _():
@@ -249,20 +256,23 @@
         new = lax.broadcasted_iota(jnp.int32, (GROUP, GROUP), 1)
         source = ((new & 127) >> 5) * 64 + (new >> 7) * 32 + (new & 31)
         perm[...] = jnp.where(old == source, 1.0, 0.0).astype(BF)
-        table = perm[...]
+        moved = perm[...].astype(F32)
         for block in range(2 * width // GROUP):
             columns = slice(block * GROUP, (block + 1) * GROUP)
-            wv[:, columns] = nn(wv[:, columns], table).astype(BF)
             row = jnp.broadcast_to(bm[:, columns], (8, GROUP))
-            bqk[:, columns] = nn(row, table.astype(F32), HI)
+            bqk[:, columns] = nn(row, moved, HI)
+
+    load_w.wait()
+
+    @pl.when(even)
+    def _():
+        moved = perm[...]
+        for block in range(2 * width // GROUP):
+            columns = slice(block * GROUP, (block + 1) * GROUP)
+            wv[:, columns] = nn(wv[:, columns], moved).astype(BF)
 
     @pl.when(s == last - 1)
     def _():
-        for k in range(n_direct, n_part):
-            down_out(k).wait_recv()
-            down_on(k).start()
-        for k in range(n_part):
-            down_send(k).start()
         cot_out.wait_recv()
         for h in range(2):
             cot_on(h).start()
@@ -344,7 +354,6 @@
     def attention_backward(i, slot):
         g_up = gin[i].astype(F32)
         gb = row_mask(i) * g_up
-        sg[6:7, :] += jnp.sum(gb, axis=0, keepdims=True)
         low = gb.astype(BF)
         dctx_all = nt(low, wv[:, 3 * width :]).astype(BF)
         for g in range(n_group):
@@ -379,12 +388,7 @@
                 turn = turn + (g2 * r[:, :128] - g1 * r[:, 128:]) * size
                 raw = jnp.concatenate([g1 * cosine + g2 * sine, g2 * cosine - g1 * sine], axis=1).astype(BF)
                 big3[i, :, lo : lo + GROUP] = raw
-                row = 3 if lo < width else 4
-                at = g * GROUP
-                sg[row : row + 1, at : at + GROUP] += jnp.sum(raw.astype(F32), axis=0, keepdims=True)
-            raw = dval.astype(BF)
-            big3[i, :, vlo : vlo + GROUP] = raw
-            sg[5:6, g * GROUP : (g + 1) * GROUP] += jnp.sum(raw.astype(F32), axis=0, keepdims=True)
+            big3[i, :, vlo : vlo + GROUP] = dval.astype(BF)
             sums = nn(tabs[i], turn, HI)
             at = g * pairs
             sg[2:3, at : at + pairs] += sums[0:1]
@@ -428,7 +432,6 @@
     def dense_backward(i, slot):
         g_up = gin[i].astype(F32)
         gb = row_mask(i) * g_up
-        sg[2:3, :] += jnp.sum(gb, axis=0, keepdims=True)
         low = gb.astype(BF)
         for k in range(ff // width):
             for m in range(width // GROUP):
@@ -436,8 +439,6 @@
                 gh = nt(low, dv[lo : lo + GROUP, :])
                 gpre = (gh * big2[i, :, lo : lo + GROUP].astype(F32)).astype(BF)
                 big3[i, :, lo : lo + GROUP] = gpre
-                at = m * GROUP
-                sg[3 + k : 4 + k, at : at + GROUP] += jnp.sum(gpre.astype(F32), axis=0, keepdims=True)
         gact = nt(big3[i], wv[...])
         gout[slot] = norm_backward(hin[i], g_up, gact).astype(BF)
         gin[i] = low
@@ -562,14 +563,30 @@
             result_send(i).start()
         pltpu.make_async_copy(hout.at[last], o_out.at[0], out_r).start()
 
-    @pl.when(even)
-    def _():
-        back = perm[...].astype(F32)
-        for block in range(2 * width // GROUP):
-            row = 3 + block * GROUP // width
-            lo = block * GROUP % width
-            part = jnp.broadcast_to(sg[row : row + 1, lo : lo + GROUP], (8, GROUP))
-            sg[row : row + 1, lo : lo + GROUP] = nt(part, back, HI)[0:1]
+    def bias_sums():
+        ones = jnp.ones((16, n_sec * tokens), BF)
+
+        def column_sum(held):
+            return nn(ones, held.reshape(n_sec * tokens, width))[0:1]
+
+        masked = column_sum(gin[...])
+        for k in range(3):
+            sg[3 + k : 4 + k, :] = column_sum(big3[:, :, k * width : (k + 1) * width])
+
+        @pl.when(odd)
+        def _():
+            sg[2:3, :] = masked
+            sg[6:7, :] = column_sum(big3[:, :, 3 * width :])
+
+        @pl.when(even)
+        def _():
+            sg[6:7, :] = masked
+            back = perm[...].astype(F32)
+            for block in range(2 * width // GROUP):
+                row = 3 + block * GROUP // width
+                lo = block * GROUP % width
+                part = jnp.broadcast_to(sg[row : row + 1, lo : lo + GROUP], (8, GROUP))
+                sg[row : row + 1, lo : lo + GROUP] = nt(part, back, HI)[0:1]
 
     my_half = pl.ds(core * n_sub, n_sub)
     their_half = pl.ds((1 - core) * n_sub, n_sub)
@@ -774,11 +791,12 @@
         def _():
             side_send(c1 - n_main).wait_recv()
 
-        @pl.when(t == 0)
-        def _():
+        @pl.when(t == 5)
+        def _():
+            bias_sums()
             small_sib.start()
 
-        @pl.when(t == 2)
+        @pl.when(t == 8)
         def _():
             small_sib.wait()
             sg[...] = sg[...] + sg_sib[...]
@@ -786,7 +804,7 @@
         for k in range(len(lines)):
             near, across, inner, outer = spots[k]
             small_near, small_across = small_copies(k)
-            at = 2 + 9 * k
+            at = 8 + 9 * k
 
             @pl.when(outer & (t == at))
             def _():

time: 228 us -> 226 us (level)
  Pallas kernels: 209 us -> 206 us
    pallas_call x1, Pallas kernels: 209 us -> 206 us  [on_device(): pl.pallas_call(functools.partial(relay, n_sec, lines, tokens, width, ff),...]
where the time goes in v5:
time: 226 us; the launch traced here: 222 us
  Pallas kernels  206 us (91%)
  other arithmetic  10.1 us (4%)
  local copies, waits for them, and re-layouts  4.3 us (2%)
    pallas_call x1, Pallas kernels, on_device(): pl.pallas_call(functools.partial(relay, n_sec, lines, tokens, width, ff),...  206 us
    broadcast_in_dim x1, other arithmetic, on_device(): gw.astype(F32)[None]  7.52 us

profile of v5, /device:TPU:0, one launch (start us, length us, event | category | flops | bytes accessed | tf_op | source)
XLA Modules:
  0.0 222.1 jit_solution(3728568951897773305)
XLA Ops:
  1.3 206.4 %shard_map.161 = (bf16[1,256,768]{2,1,0:T(8,128)(2,1)}, bf16[1,256,768]{2,1,0:T(8,128)(2,1)}, bf16[768,3072]{1,0:T(8,128)(2,1)}, bf16[1536,768]{1,0:T(8,128)(2,1)}, f32[8,768]{1,0:T(8,128)}) custom-call(bf16[1,256,768]{2,1,0:T(8,128)(2,1)} %patches.1, bf16[1,256,768]{2,1,0:T(8,128)(2,1)} %cot.1, s32[1,2,256]{2,1,0:T(2,128)} %positions.1, ...), custom_call_target="tpu_custom_call" | custom-call | tf_op jit(solution)/shard_map/pallas_call | solution.py:1081
  207.7 1.4 fusion
  209.1 0.7 slice_bitcast_fusion
  209.9 0.6 copy.18
  210.5 0.0 copy-start
  210.5 7.5 %bitcast_convert_fusion = f32[1,768,3072]{2,1,0:T(8,128)} fusion(bf16[768,3072]{1,0:T(8,128)(2,1)} %get-tuple-element.16), kind=kLoop, calls=%fused_computation | loop fusion | flops 2359296 | bytes 14155776 | tf_op jit(solution)/shard_map/broadcast_in_dim | solution.py:1102
  218.0 0.0 copy-start.2
  218.0 0.0 copy-start.1
  218.0 0.0 copy-done
  218.0 2.5 %bitcast_convert_fusion.1 = f32[1,1536,768]{2,1,0:T(8,128)} fusion(bf16[1536,768]{1,0:T(8,128)(2,1)S(1)} %copy-done), kind=kLoop, calls=%fused_computation.1 | loop fusion | flops 1179648 | bytes 7077888 | tf_op jit(solution)/shard_map/broadcast_in_dim | solution.py:1105
  220.6 0.0 copy-done.2
  220.6 0.7 copy.22
  221.3 0.0 copy-done.1
  221.3 0.7 copy.23
Async XLA Ops:
  210.5 7.5 %copy-start = (bf16[1536,768]{1,0:T(8,128)(2,1)S(1)}, bf16[1536,768]{1,0:T(8,128)(2,1)}, u32[]{:S(2)}) copy-start(bf16[1536,768]{1,0:T(8,128)(2,1)} %get-tuple-element.17) | copy-start | bytes 7077892
  218.0 2.6 %copy-start.2 = (bf16[1,256,768]{2,1,0:T(8,128)(2,1)S(1)}, bf16[1,256,768]{2,1,0:T(8,128)(2,1)}, u32[]{:S(2)}) copy-start(bf16[1,256,768]{2,1,0:T(8,128)(2,1)} %get-tuple-element.29) | copy-start | bytes 1179652
  218.0 3.3 %copy-start.1 = (bf16[1,256,768]{2,1,0:T(8,128)(2,1)S(1)}, bf16[1,256,768]{2,1,0:T(8,128)(2,1)}, u32[]{:S(2)}) copy-start(bf16[1,256,768]{2,1,0:T(8,128)(2,1)} %get-tuple-element.30) | copy-start | bytes 1179652

commit v6 on v5

--- a/solution.py
+++ b/solution.py
@@ -340,8 +340,11 @@
             context = nn(jnp.concatenate(weights, axis=1), stacked)
             lo = 3 * width + g * GROUP
             big1[i, :, lo : lo + GROUP] = context.astype(BF)
-        branch = nn(big1[i, :, 3 * width :], wv[:, 3 * width :]) + bm[:, 3 * width :]
-        hout[slot] = (x + row_mask(i) * branch).astype(BF)
+        for h in range(2):
+            r = slice(h * half, (h + 1) * half)
+            branch = nn(big1[i, r, 3 * width :], wv[:, 3 * width :]) + bm[:, 3 * width :]
+            hout[slot, r] = (x[r] + row_mask(i)[r] * branch).astype(BF)
+            send_hop(i, h)
 
     def norm_backward(x, g_up, gact):
         xhat, scale = normalise(x.astype(F32))
@@ -483,8 +486,6 @@
             for h in range(2):
                 hop_send(i, h).wait_recv()
             attention_forward(i, i)
-            for h in range(2):
-                send_hop(i, h)
 
         @pl.when(odd)
         def _():

time: 226 us -> 226 us (level)
  no operation moved by 1% of the time
where the time goes in v6:
time: 226 us; the launch traced here: 222 us
  Pallas kernels  206 us (91%)
  other arithmetic  10.1 us (4%)
  local copies, waits for them, and re-layouts  4.3 us (2%)
    pallas_call x1, Pallas kernels, on_device(): pl.pallas_call(functools.partial(relay, n_sec, lines, tokens, width, ff),...  206 us
    broadcast_in_dim x1, other arithmetic, on_device(): gw.astype(F32)[None]  7.52 us

profile of v6, /device:TPU:0, one launch (start us, length us, event | category | flops | bytes accessed | tf_op | source)
XLA Modules:
  0.0 222.0 jit_solution(13763815060225497948)
XLA Ops:
  1.3 206.4 %shard_map.161 = (bf16[1,256,768]{2,1,0:T(8,128)(2,1)}, bf16[1,256,768]{2,1,0:T(8,128)(2,1)}, bf16[768,3072]{1,0:T(8,128)(2,1)}, bf16[1536,768]{1,0:T(8,128)(2,1)}, f32[8,768]{1,0:T(8,128)}) custom-call(bf16[1,256,768]{2,1,0:T(8,128)(2,1)} %patches.1, bf16[1,256,768]{2,1,0:T(8,128)(2,1)} %cot.1, s32[1,2,256]{2,1,0:T(2,128)} %positions.1, ...), custom_call_target="tpu_custom_call" | custom-call | tf_op jit(solution)/shard_map/pallas_call | solution.py:1082
  207.7 1.4 fusion
  209.1 0.7 slice_bitcast_fusion
  209.9 0.6 copy.18
  210.5 0.0 copy-start
  210.5 7.5 %bitcast_convert_fusion = f32[1,768,3072]{2,1,0:T(8,128)} fusion(bf16[768,3072]{1,0:T(8,128)(2,1)} %get-tuple-element.16), kind=kLoop, calls=%fused_computation | loop fusion | flops 2359296 | bytes 14155776 | tf_op jit(solution)/shard_map/broadcast_in_dim | solution.py:1103
  218.0 0.0 copy-start.2
  218.0 0.0 copy-start.1
  218.0 0.0 copy-done
  218.0 2.5 %bitcast_convert_fusion.1 = f32[1,1536,768]{2,1,0:T(8,128)} fusion(bf16[1536,768]{1,0:T(8,128)(2,1)S(1)} %copy-done), kind=kLoop, calls=%fused_computation.1 | loop fusion | flops 1179648 | bytes 7077888 | tf_op jit(solution)/shard_map/broadcast_in_dim | solution.py:1106
  220.5 0.0 copy-done.2
  220.5 0.7 copy.22
  221.3 0.0 copy-done.1
  221.3 0.7 copy.23
Async XLA Ops:
  210.5 7.5 %copy-start = (bf16[1536,768]{1,0:T(8,128)(2,1)S(1)}, bf16[1536,768]{1,0:T(8,128)(2,1)}, u32[]{:S(2)}) copy-start(bf16[1536,768]{1,0:T(8,128)(2,1)} %get-tuple-element.17) | copy-start | bytes 7077892
  218.0 2.6 %copy-start.2 = (bf16[1,256,768]{2,1,0:T(8,128)(2,1)S(1)}, bf16[1,256,768]{2,1,0:T(8,128)(2,1)}, u32[]{:S(2)}) copy-start(bf16[1,256,768]{2,1,0:T(8,128)(2,1)} %get-tuple-element.29) | copy-start | bytes 1179652
  218.0 3.3 %copy-start.1 = (bf16[1,256,768]{2,1,0:T(8,128)(2,1)S(1)}, bf16[1,256,768]{2,1,0:T(8,128)(2,1)}, u32[]{:S(2)}) copy-start(bf16[1,256,768]{2,1,0:T(8,128)(2,1)} %get-tuple-element.30) | copy-start | bytes 1179652
